TPU v7x, 256 devices: a whole 4x4x8 slice. The times are simulated.
256 devices in a mesh: ctx: 64 (over x, z, core), head: 4 (over y).
Axes of the slice: x: 4, y: 4, z: 8, core: 2. Of those that a mesh axis runs over, the one named last changes fastest.
Arguments:
- queries: bfloat16 [16384, 4096], P('ctx', 'head'), may hold values from -6 to 6
- key_rows: bfloat16 [16384, 4096], P('ctx', 'head'), may hold values from -3 to 3
- value_rows: bfloat16 [16384, 4096], P('ctx', 'head'), may hold values from -12 to 12
- gate_logits: bfloat16 [16384, 4096], P('ctx', 'head'), may hold values from -6 to 6
- norm_gain: float32 [4096], P('head'), may hold values from 0.5 to 1.5
- log_decay: float32 [16384, 32], P('ctx', 'head')
- cotangent: bfloat16 [16384, 4096], P('ctx', 'head'), may hold values from -6 to 6
Outputs:
- attended: bfloat16 [16384, 4096], P('ctx', 'head')
- grad_queries: bfloat16 [16384, 4096], P('ctx', 'head')
- grad_keys: bfloat16 [16384, 4096], P('ctx', 'head')
- grad_values: bfloat16 [16384, 4096], P('ctx', 'head')
- grad_gate: bfloat16 [16384, 4096], P('ctx', 'head')
- grad_decay: float32 [16384, 32], P('ctx', 'head')
- grad_gain: float32 [4096], P('head')
All inputs are finite; a program needn't handle non-finite values.
Results may differ from a plain program's by a relative error of at most 0.0069.
Values may be sent and summed in bfloat16 or wider, within the bound.
No kernel may reach another device: no remote copies, remote signals or barrier semaphores. Data moves between devices by JAX's collectives and lax.ppermute only.
A program may use at most 192 MiB of HBM per device.

v0:
```python
import jax
import jax.numpy as jnp
from jax import lax
from jax.sharding import PartitionSpec as P

EPSILON = 1e-05


def carried_in(value, axis, join, neutral, backward):
    count, mine = (lax.axis_size(axis), lax.axis_index(axis))
    pieces = jax.tree.map(lambda part: lax.all_gather(part, axis), value)
    if backward:
        pieces = jax.tree.map(lambda part: part[::-1], pieces)
        mine = count - 1 - mine
    subtotal = jax.tree.map(
        lambda part, zero: jnp.full_like(part, 0) + jnp.asarray(zero, part.dtype), value, neutral
    )

    def turn(position, subtotal):
        longer = join(subtotal, jax.tree.map(lambda part: part[position], pieces))
        return jax.tree.map(lambda new, old: jnp.where(position < mine, new, old), longer, subtotal)

    return lax.fori_loop(0, count - 1, turn, subtotal)


def combine_states(earlier, later):
    return (earlier[0] * later[0], later[0][:, None, None] * earlier[1] + later[1])


def lower_ones(length):
    row_iota = lax.broadcasted_iota(jnp.int32, (length, length), 0)
    col_iota = lax.broadcasted_iota(jnp.int32, (length, length), 1)
    return (col_iota <= row_iota).astype(jnp.float32)


def per_device(queries, key_rows, value_rows, gate_logits, norm_gain, log_decay, cotangent):
    row_count = queries.shape[0]
    width_here = queries.shape[1]
    heads_here = log_decay.shape[1]
    head_size = width_here // heads_here
    full_width = width_here * lax.axis_size("head")
    query_heads = queries.reshape(row_count, heads_here, head_size)
    key_heads = key_rows.reshape(row_count, heads_here, head_size)
    value_heads = value_rows.reshape(row_count, heads_here, head_size)
    triangle = lower_ones(row_count)
    cumulative = jnp.dot(
        triangle, log_decay, precision=lax.Precision.HIGHEST, preferred_element_type=jnp.float32
    )
    last_log = cumulative[row_count - 1]
    causal = (triangle > 0.5)[None]
    log_gap = cumulative.T[:, :, None] - cumulative.T[:, None, :]
    decay_mask = jnp.where(causal, jnp.exp(jnp.where(causal, log_gap, 0.0)), 0.0)
    scores = jnp.einsum("ihd,jhd->hij", query_heads, key_heads, preferred_element_type=jnp.float32)
    weights = (decay_mask * scores).astype(jnp.bfloat16)
    intra_sum = jnp.einsum("hij,jhe->ihe", weights, value_heads, preferred_element_type=jnp.float32)
    query_decayed = (query_heads * jnp.exp(cumulative)[:, :, None]).astype(jnp.bfloat16)
    key_fade = jnp.exp(last_log[None, :] - cumulative)
    key_decayed = (key_heads * key_fade[:, :, None]).astype(jnp.bfloat16)
    local_state = jnp.einsum(
        "jhd,jhe->hde", key_decayed, value_heads, preferred_element_type=jnp.float32
    ).astype(jnp.bfloat16)
    block_decay = jnp.exp(last_log)
    widened = lax.optimization_barrier(local_state).astype(jnp.float32)
    start_pair = (jnp.ones_like(block_decay), jnp.zeros_like(widened))
    _, prior_state = carried_in((block_decay, widened), "ctx", combine_states, start_pair, False)
    prior_bf = prior_state.astype(jnp.bfloat16)
    inter_sum = jnp.einsum(
        "ihd,hde->ihe", query_decayed, prior_bf, preferred_element_type=jnp.float32
    )
    attention = (intra_sum + inter_sum).reshape(row_count, width_here)
    gate_open = jax.nn.sigmoid(gate_logits.astype(jnp.float32))
    upstream = cotangent.astype(jnp.float32)
    gain_row = norm_gain[None, :]
    through_gate = upstream * gate_open
    squares = lax.psum(jnp.sum(attention * attention, axis=1), "head")
    root_mean = jnp.sqrt(squares / full_width + EPSILON)
    normalized = attention / root_mean[:, None]
    cross_dot = lax.psum(jnp.sum(through_gate * gain_row * normalized, axis=1), "head")
    scaled = normalized * gain_row
    attended = (scaled * gate_open).astype(jnp.bfloat16)
    grad_gate = (upstream * scaled * gate_open * (1.0 - gate_open)).astype(jnp.bfloat16)
    grad_gain = lax.psum(jnp.sum(through_gate * normalized, axis=0), "ctx")
    grad_attention = (
        (through_gate * gain_row - normalized * (cross_dot / full_width)[:, None])
        / root_mean[:, None]
    ).astype(jnp.bfloat16)
    grad_attention = grad_attention.reshape(row_count, heads_here, head_size)
    outgoing = jnp.einsum(
        "ihd,ihe->hde", query_decayed, grad_attention, preferred_element_type=jnp.float32
    )
    end_pair = (jnp.ones_like(block_decay), jnp.zeros_like(outgoing))
    _, later_state = carried_in((block_decay, outgoing), "ctx", combine_states, end_pair, True)
    later_bf = later_state.astype(jnp.bfloat16)
    grad_scores = jnp.einsum(
        "ihe,jhe->hij", grad_attention, value_heads, preferred_element_type=jnp.float32
    )
    products = decay_mask * scores * grad_scores
    mixed = (decay_mask * grad_scores).astype(jnp.bfloat16)
    grad_q = jnp.einsum("hij,jhd->ihd", mixed, key_heads, preferred_element_type=jnp.float32)
    grad_q = grad_q + jnp.exp(cumulative)[:, :, None] * jnp.einsum(
        "ihe,hde->ihd", grad_attention, prior_bf, preferred_element_type=jnp.float32
    )
    value_pull = jnp.einsum(
        "jhe,hde->jhd", value_heads, later_bf, preferred_element_type=jnp.float32
    )
    key_pull = jnp.einsum("jhd,hde->jhe", key_heads, later_bf, preferred_element_type=jnp.float32)
    grad_k = (
        jnp.einsum("hij,ihd->jhd", mixed, query_heads, preferred_element_type=jnp.float32)
        + key_fade[:, :, None] * value_pull
    )
    grad_v = (
        jnp.einsum("hij,ihe->jhe", weights, grad_attention, preferred_element_type=jnp.float32)
        + key_fade[:, :, None] * key_pull
    )
    state_pull = key_fade * jnp.sum(key_heads * value_pull, axis=2)
    grad_cum = (
        jnp.sum(inter_sum * grad_attention, axis=2)
        + jnp.sum(products, axis=2).T
        - jnp.sum(products, axis=1).T
        - state_pull
    )
    tail_term = jnp.sum(state_pull, axis=0) + block_decay * jnp.sum(
        later_state * prior_state, axis=(1, 2)
    )
    is_last = lax.broadcasted_iota(jnp.int32, (row_count, 1), 0) == row_count - 1
    grad_cum = grad_cum + jnp.where(is_last, tail_term[None, :], 0.0)
    grad_decay = jnp.dot(
        triangle.T, grad_cum, precision=lax.Precision.HIGHEST, preferred_element_type=jnp.float32
    )
    return (
        attended,
        grad_q.astype(jnp.bfloat16).reshape(row_count, width_here),
        grad_k.astype(jnp.bfloat16).reshape(row_count, width_here),
        grad_v.astype(jnp.bfloat16).reshape(row_count, width_here),
        grad_gate,
        grad_decay,
        grad_gain,
    )


def solution(mesh):
    return jax.shard_map(
        per_device,
        mesh=mesh,
        in_specs=(
            P("ctx", "head"),
            P("ctx", "head"),
            P("ctx", "head"),
            P("ctx", "head"),
            P("head"),
            P("ctx", "head"),
            P("ctx", "head"),
        ),
        out_specs=(
            P("ctx", "head"),
            P("ctx", "head"),
            P("ctx", "head"),
            P("ctx", "head"),
            P("ctx", "head"),
            P("ctx", "head"),
            P("head"),
        ),
        check_vma=False,
    )
```

profile of v0, /device:TPU:1, one launch (start us, length us, event | category | flops | bytes accessed | tf_op | source)
XLA Modules:
  0.0 518.3 jit_solution(16922923870495869831)
XLA Ops:
  8.5 1.3 copy.59
  12.0 44.0 %all-gather.2 = f32[64,1,8]{2,1,0:T(1,128)S(1)} all-gather(f32[1,1,8]{2,1,0:T(1,128)S(1)} %bitcast.142), channel_id=1, replica_groups=mesh['ctx'=64,'head'=4] {'ctx'}, dimensions={0}, use_global_device_ids=true | all-gather | bytes 2080 | tf_op jit(solution)/shard_map/all_gather | solution.py:11
  56.1 1.9 fusion.2
  58.0 99.7 %all-gather.6.cloned.1.call-done = f32[512,128,128]{2,1,0:T(8,128)} async-done(((f32[8,128,128]{2,1,0:T(8,128)}), f32[512,128,128]{2,1,0:T(8,128)}) %all-gather.6.cloned.1.call-update) | async-done | bytes 33554448 | tf_op jit(solution)/shard_map/all_gather | solution.py:11
  157.8 76.7 %while.28 = (s32[]{:T(128)}, f32[8,128,128]{2,1,0:T(8,128)S(1)}, s32[]{:T(128)}, f32[64,8]{1,0:T(8,128)S(1)}, f32[64,8,128,128]{3,2,1,0:T(8,128)}, /*index=5*/s32[]{:T(128)}, s32[]{:T(128)}) while((s32[]{:T(128)}, f32[8,128,128]{2,1,0:T(8,128)S(1)}, s32[]{:T(128)}, f32[64,8]{1,0:T(8,128)S(1)}, f32[64,8,128,128]{3,2,1,0:T(8,128)}, ...), condition=%wide.region_1.2_spmd.clone, body=%wide.region_0.1_spmd.clone.sunk | while | flops 524292 | bytes 1573073 | solution.py:23
  234.4 1.4 convolution_bitcast_fusion.3
  235.9 1.5 multiply_reduce_fusion.3
  237.4 8.6 %psum.21 = f32[256]{0:T(256)S(1)} all-reduce(f32[256]{0:T(256)S(1)} %get-tuple-element.285), channel_id=1, replica_groups=mesh['ctx'=64,'head'=4] {'head'}, use_global_device_ids=true, to_apply=%region_3.4 | all-reduce | flops 256 | bytes 2048 | tf_op jit(solution)/shard_map/psum | solution.py:75
  246.0 1.6 copy.66
  248.1 6.0 %psum.22 = f32[256]{0:T(256)S(1)} all-reduce(f32[256]{0:T(256)S(1)} %get-tuple-element.257), channel_id=1, replica_groups=mesh['ctx'=64,'head'=4] {'head'}, use_global_device_ids=true, to_apply=%region_5.6 | all-reduce | flops 256 | bytes 2048 | tf_op jit(solution)/shard_map/psum | solution.py:78
  254.2 2.9 fusion.16
  257.1 1.2 copy.67
  259.5 2.3 multiply_reduce_fusion.5
  264.2 2.0 copy.77
  266.3 130.2 %psum.23 = f32[1024]{0:T(1024)} all-reduce(f32[1024]{0:T(1024)S(1)} %get-tuple-element.256), channel_id=1, replica_groups=mesh['ctx'=64,'head'=4] {'ctx'}, use_global_device_ids=true, to_apply=%region_15.16 | all-reduce | flops 1024 | bytes 8192 | tf_op jit(solution)/shard_map/psum | solution.py:82
  396.5 2.0 convolution_bitcast_fusion.5
  398.5 3.5 all-gather.8.cloned.1.call-done
  402.0 23.0 %rev.7 = f32[64,8,128,128]{3,2,1,0:T(8,128)} reverse(f32[64,8,128,128]{3,2,1,0:T(8,128)} %bitcast.120), dimensions={0} | reverse | bytes 67108864 | tf_op jit(solution)/shard_map/rev | solution.py:13
  425.0 76.9 %while.29 = (s32[]{:T(128)}, f32[8,128,128]{2,1,0:T(8,128)S(1)}, s32[]{:T(128)}, f32[64,8]{1,0:T(8,128)S(1)}, f32[64,8,128,128]{3,2,1,0:T(8,128)}, /*index=5*/s32[]{:T(128)}, s32[]{:T(128)}) while((s32[]{:T(128)}, f32[8,128,128]{2,1,0:T(8,128)S(1)}, s32[]{:T(128)}, f32[64,8]{1,0:T(8,128)S(1)}, f32[64,8,128,128]{3,2,1,0:T(8,128)}, ...), condition=%wide.region_7.8_spmd.clone, body=%wide.region_6.7_spmd.clone.sunk | while | flops 524292 | bytes 1573073 | solution.py:23
  425.0 1.2 fusion.64
  426.3 1.2 fusion.64
  427.5 1.2 fusion.64
  428.7 1.2 fusion.64
  438.5 1.2 fusion.64
  442.1 1.2 fusion.64
  461.6 1.2 fusion.64
  465.3 1.2 fusion.64
  484.8 1.2 fusion.64
  488.5 1.2 fusion.64
  502.0 1.3 fusion.13
  504.5 2.0 copy.79
  506.6 2.6 fusion.9
  (300 shorter events, 149.1 us)
Async XLA Ops:
  7.2 2.6 copy-start
  7.2 3.9 copy-start.12
  7.2 150.6 %all-gather.6.cloned.1.call-start = ((), (), s32[]{:S(2)}) async-start(), calls=%async_computation | async-start | bytes 34078720 | tf_op jit(solution)/shard_map/all_gather | solution.py:11
  9.8 1.2 copy-start.4
  11.0 391.0 %all-gather.8.cloned.1.call-start = ((), (), s32[]{:S(2)}) async-start(), calls=%async_computation.1 | async-start | bytes 34078720 | tf_op jit(solution)/shard_map/all_gather | solution.py:11
  58.0 177.8 %copy-start.1 = (f32[8,256,256]{2,1,0:T(8,128)}, f32[8,256,256]{2,1,0:T(8,128)S(1)}, u32[]{:S(2)}) copy-start(f32[8,256,256]{2,1,0:T(8,128)S(1)} %fusion.2) | copy-start | bytes 6291460
  235.9 1.5 copy-start.2
  237.4 10.2 %copy-start.10 = (bf16[256,1024]{1,0:T(8,128)(2,1)S(1)}, bf16[256,1024]{1,0:T(8,128)(2,1)}, u32[]{:S(2)}) copy-start(bf16[256,1024]{1,0:T(8,128)(2,1)} %param.17) | copy-start | bytes 1572868
  237.4 10.2 %copy-start.11 = (bf16[256,1024]{1,0:T(8,128)(2,1)S(1)}, bf16[256,1024]{1,0:T(8,128)(2,1)}, u32[]{:S(2)}) copy-start(bf16[256,1024]{1,0:T(8,128)(2,1)} %param.14) | copy-start | bytes 1572868
  237.4 10.2 %copy-start.13 = (f32[1024]{0:T(1024)S(1)}, f32[1024]{0:T(1024)}, u32[]{:S(2)}) copy-start(f32[1024]{0:T(1024)} %param.15) | copy-start | bytes 12292
  254.2 4.2 copy-start.7
  259.5 2.3 copy-start.5
  261.8 1.4 copy-start.9
  263.1 133.3 %copy-start.3 = (f32[256,8,128]{0,2,1:T(8,128)S(1)}, f32[256,8,128]{0,2,1:T(8,128)}, u32[]{:S(2)}) copy-start(f32[256,8,128]{0,2,1:T(8,128)} %copy-done.2) | copy-start | bytes 3145732
  425.0 77.0 %copy-start.6 = (bf16[256,1024]{0,1:T(8,128)(2,1)S(1)}, bf16[256,1024]{0,1:T(8,128)(2,1)}, u32[]{:S(2)}) copy-start(bf16[256,1024]{0,1:T(8,128)(2,1)} %copy-done.4) | copy-start | bytes 1572868
  503.3 3.3 copy-start.8
Sparse Core Ops, SparseCore 0:
  11.4 146.3 all-gather.5
  259.6 142.3 all-gather.7
where the time goes:
time: 525 us; the launch traced here: 518 us
  blocking collectives  189 us (36%)
  other arithmetic  153 us (29%)
  waiting for transfers between devices  103 us (20%)
  local copies, waits for them, and re-layouts  35.4 us (7%)
  matrix products  19.1 us (4%)
  between operations  14.3 us (3%)
    select_n x126, other arithmetic, turn(): jnp.where(position < mine, new, old)  148 us
    psum x1, blocking collectives, per_device(): grad_gain = lax.psum(jnp.sum(through_gate * normalized, axis=0), 'ctx')  130 us
    all_gather x2, waiting for transfers between devices, carried_in(): pieces = jax.tree.map(lambda part: lax.all_gather(part, axis), value)  103 us
    all_gather x1, blocking collectives, carried_in(): pieces = jax.tree.map(lambda part: lax.all_gather(part, axis), value)  44 us
    rev x2, local copies, waits for them, and re-layouts, carried_in(): pieces = jax.tree.map(lambda part: part[::-1], pieces)  23 us
  transfers between devices with their start and end apart: 2, of which 2 were waited for; matrix products, arithmetic and copies ran while one was open for 2% of the time, Pallas kernels for 0%

commit v1 on v0

v1 whole, which is shorter than its diff:
```python
import functools

import jax
import jax.numpy as jnp
from jax import lax
from jax.experimental import pallas as pl
from jax.experimental.pallas import tpu as pltpu
from jax.sharding import PartitionSpec as P

EPSILON = 1e-05
HD = 128
ROWS = 16
EXTRA = 8
F32 = jnp.float32
BF16 = jnp.bfloat16
NEGATIVE = -1e30


def dot(a, b, contract=(1, 0)):
    dims = (((contract[0],), (contract[1],)), ((), ()))
    return lax.dot_general(a, b, dims, preferred_element_type=F32)


def three_parts(value):
    high = value.astype(BF16)
    rest = value - high.astype(F32)
    middle = rest.astype(BF16)
    low = (rest - middle.astype(F32)).astype(BF16)
    return high, middle, low


def triangle_bf(length, flipped=False):
    row = lax.broadcasted_iota(jnp.int32, (length, length), 0)
    col = lax.broadcasted_iota(jnp.int32, (length, length), 1)
    return jnp.where(row <= col if flipped else col <= row, 1.0, 0.0).astype(BF16)


def exact_sums(ones, value):
    return sum(dot(ones, part) for part in three_parts(value))


def small_rows(value):
    high, middle, low = (part.astype(F32) for part in three_parts(value))
    row = lax.broadcasted_iota(jnp.int32, (EXTRA, HD), 0)
    block = jnp.where(row == 0, high, jnp.where(row == 1, middle, jnp.where(row == 2, low, 0.0)))
    return block.astype(BF16)


def joined_rows(block):
    block = block.astype(F32)
    return block[0:1] + block[1:2] + block[2:3]


def masked_gap(cum_col, cum_row, low, high, left, right):
    gap = cum_col[low:high] - cum_row[:, left:right]
    if right <= low:
        return gap
    row = lax.broadcasted_iota(jnp.int32, gap.shape, 0) + low
    col = lax.broadcasted_iota(jnp.int32, gap.shape, 1) + left
    return jnp.where(col <= row, gap, NEGATIVE)


def decay_blocks(cum_col, cum_row):
    length = cum_col.shape[0]
    half = length // 2
    top = jnp.exp(masked_gap(cum_col, cum_row, 0, half, 0, half))
    bottom = jnp.exp(masked_gap(cum_col, cum_row, half, length, 0, length))
    return top, bottom


def local_state_kernel(heads, k_ref, v_ref, ld_ref, pay_ref, cum_ref, cumt_ref, loc_ref):
    length = k_ref.shape[0]
    cum = exact_sums(triangle_bf(length), ld_ref[...])
    cum_ref[...] = cum
    wide = jnp.concatenate([cum, jnp.zeros((length, HD - heads), F32)], axis=1)
    cumt_ref[...] = wide.T[:heads]
    last = cum[length - 1 : length]
    fade = jnp.exp(last - cum)
    for h in range(heads):
        cols = slice(h * HD, (h + 1) * HD)
        decayed = (k_ref[:, cols].astype(F32) * fade[:, h : h + 1]).astype(BF16)
        state = dot(decayed, v_ref[:, cols], (0, 0)).astype(BF16)
        loc_ref[h] = state
        rows = small_rows(jnp.broadcast_to(last[:, h : h + 1], (1, HD)))
        for part in range(HD // ROWS):
            pay_ref[h * (HD // ROWS) + part, :ROWS] = state[part * ROWS : (part + 1) * ROWS]
            pay_ref[h * (HD // ROWS) + part, ROWS:] = rows


def forward_scan_kernel(pay_ref, out_ref, decay_ref):
    state = jnp.zeros((ROWS, HD), F32)
    for c in range(pay_ref.shape[0]):
        out_ref[c] = state.astype(BF16)
        decay = jnp.exp(joined_rows(pay_ref[c, ROWS:]))
        decay_ref[c : c + 1] = decay
        state = decay * state + pay_ref[c, :ROWS].astype(F32)


def backward_scan_kernel(pay_ref, decay_ref, out_ref):
    state = jnp.zeros((ROWS, HD), F32)
    total = jnp.zeros((1, HD), F32)
    for c in reversed(range(pay_ref.shape[0])):
        out_ref[c, :ROWS] = state.astype(BF16)
        state = decay_ref[c : c + 1] * state + pay_ref[c, :ROWS].astype(F32)
        total = total + joined_rows(pay_ref[c, ROWS:])
    rows = small_rows(total)
    for c in range(pay_ref.shape[0]):
        out_ref[c, ROWS:] = rows


def attention_kernel(
    heads, q_ref, k_ref, v_ref, gate_ref, cot_ref, gain_ref, cum_ref, cumt_ref, prior_ref,
    attn_ref, weights_ref, sums_ref,
):
    length = q_ref.shape[0]
    half = length // 2
    squares = jnp.zeros((length, HD), F32)
    cross = jnp.zeros((length, HD), F32)
    cum = cum_ref[...]
    for h in range(heads):
        cols = slice(h * HD, (h + 1) * HD)
        q, k, v = q_ref[:, cols], k_ref[:, cols], v_ref[:, cols]
        top, bottom = decay_blocks(cum[:, h : h + 1], cumt_ref[h : h + 1])
        top = (top * dot(q[:half], k[:half], (1, 1))).astype(BF16)
        bottom = (bottom * dot(q[half:], k, (1, 1))).astype(BF16)
        weights_ref[h, :half, :half] = top
        weights_ref[h, :half, half:] = jnp.zeros((half, length - half), BF16)
        weights_ref[h, half:] = bottom
        decayed = (q.astype(F32) * jnp.exp(cum[:, h : h + 1])).astype(BF16)
        attn = dot(decayed, prior_ref[h]) + jnp.concatenate([dot(top, v[:half]), dot(bottom, v)])
        attn_ref[:, cols] = attn
        opened = jax.nn.sigmoid(gate_ref[:, cols].astype(F32))
        upstream = cot_ref[:, cols].astype(F32) * opened * gain_ref[:, cols]
        squares = squares + attn * attn
        cross = cross + upstream * attn
    sums_ref[...] = jnp.concatenate(
        [
            jnp.sum(squares.T, axis=0, keepdims=True),
            jnp.sum(cross.T, axis=0, keepdims=True),
            jnp.zeros((6, length), F32),
        ]
    )


def norm_kernel(
    heads, full_width, q_ref, gate_ref, cot_ref, gain_ref, cum_ref, attn_ref, *rest
):
    sums_refs, (attended_ref, ggate_ref, grad_ref, pay_ref) = rest[:-4], rest[-4:]
    length = q_ref.shape[0]
    sums = sum(ref[...] for ref in sums_refs)
    inverse_row = 1.0 / jnp.sqrt(sums[0:1] / full_width + EPSILON)
    cross_row = sums[1:2] * inverse_row / full_width
    inverse = jnp.broadcast_to(inverse_row, (HD, length)).T
    cross = jnp.broadcast_to(cross_row, (HD, length)).T
    cum = cum_ref[...]
    for h in range(heads):
        cols = slice(h * HD, (h + 1) * HD)
        opened = jax.nn.sigmoid(gate_ref[:, cols].astype(F32))
        through = cot_ref[:, cols].astype(F32) * opened
        gain = gain_ref[:, cols]
        normalized = attn_ref[:, cols] * inverse
        scaled = normalized * gain
        attended_ref[:, cols] = (scaled * opened).astype(BF16)
        ggate_ref[:, cols] = (through * scaled * (1.0 - opened)).astype(BF16)
        gain_sum = jnp.sum(through * normalized, axis=0, keepdims=True)
        grad = ((through * gain - normalized * cross) * inverse).astype(BF16)
        grad_ref[:, cols] = grad
        decayed = (q_ref[:, cols].astype(F32) * jnp.exp(cum[:, h : h + 1])).astype(BF16)
        outgoing = dot(decayed, grad, (0, 0)).astype(BF16)
        rows = small_rows(gain_sum)
        for part in range(HD // ROWS):
            pay_ref[h * (HD // ROWS) + part, :ROWS] = outgoing[part * ROWS : (part + 1) * ROWS]
            pay_ref[h * (HD // ROWS) + part, ROWS:] = rows


def gradient_kernel(
    heads, q_ref, k_ref, v_ref, cum_ref, cumt_ref, weights_ref, attn_ref, grad_ref, prior_ref,
    loc_ref, back_ref, gq_ref, gk_ref, gv_ref, gdecay_ref, ggain_ref,
):
    length = q_ref.shape[0]
    half = length // 2
    parts = HD // ROWS
    cum = cum_ref[...]
    last = cum[length - 1 : length]
    lane = lax.broadcasted_iota(jnp.int32, (1, HD), 1)
    tails = jnp.zeros((1, HD), F32)
    columns = []
    for h in range(heads):
        cols = slice(h * HD, (h + 1) * HD)
        q, k, v, grad = q_ref[:, cols], k_ref[:, cols], v_ref[:, cols], grad_ref[:, cols]
        prior = prior_ref[h]
        later = jnp.concatenate([back_ref[h * parts + part, :ROWS] for part in range(parts)])
        ggain_ref[:, cols] = joined_rows(back_ref[h * parts, ROWS:])
        top, bottom = decay_blocks(cum[:, h : h + 1], cumt_ref[h : h + 1])
        top = (top * dot(grad[:half], v[:half], (1, 1))).astype(BF16)
        bottom = (bottom * dot(grad[half:], v, (1, 1))).astype(BF16)
        gq = jnp.concatenate([dot(top, k[:half]), dot(bottom, k)])
        gq = gq + jnp.exp(cum[:, h : h + 1]) * dot(grad, prior, (1, 1))
        gq_ref[:, cols] = gq.astype(BF16)
        mixed = jnp.concatenate(
            [jnp.concatenate([top, jnp.zeros((half, length - half), BF16)], axis=1), bottom]
        )
        fade = jnp.exp(last[:, h : h + 1] - cum[:, h : h + 1])
        gk = dot(mixed, q, (0, 0)) + fade * dot(v, later, (1, 1))
        gk_ref[:, cols] = gk.astype(BF16)
        gv = dot(weights_ref[h], grad, (0, 0)) + fade * dot(k, later)
        gv_ref[:, cols] = gv.astype(BF16)
        following = loc_ref[h].astype(F32) + jnp.exp(last[:, h : h + 1]) * prior.astype(F32)
        tail = jnp.sum(following * later.astype(F32))
        tails = jnp.where(lane == h, tail, tails)
        change = attn_ref[:, cols] * grad.astype(F32) - k.astype(F32) * gk
        columns.append(jnp.sum(change, axis=1, keepdims=True))
    change = jnp.concatenate(columns, axis=1)
    gdecay_ref[...] = exact_sums(triangle_bf(length, True), change) + tails[:, :heads]


def local_call(kernel, outs, args, flops=0, moved=0):
    return pl.pallas_call(
        kernel,
        out_shape=[jax.ShapeDtypeStruct(shape, kind) for shape, kind in outs],
        compiler_params=pltpu.CompilerParams(vmem_limit_bytes=48 * 2**20),
    )(*args)


def exchange(payload):
    return lax.all_to_all(payload, "ctx", 0, 0, tiled=True)


def per_device(queries, key_rows, value_rows, gate_logits, norm_gain, log_decay, cotangent):
    length, width = queries.shape
    heads = log_decay.shape[1]
    count = lax.axis_size("ctx")
    full_width = width * lax.axis_size("head")
    gain = norm_gain.reshape(1, width)
    state = (heads, HD, HD)
    chunks = heads * HD // ROWS
    payload, cum, cumt, local = local_call(
        functools.partial(local_state_kernel, heads),
        [((chunks, ROWS + EXTRA, HD), BF16), ((length, heads), F32), ((heads, length), F32), (state, BF16)],
        (key_rows, value_rows, log_decay),
    )
    arrived = exchange(payload)
    scanned, decays = local_call(
        forward_scan_kernel, [((count, ROWS, HD), BF16), ((count, HD), F32)], (arrived,)
    )
    prior = exchange(scanned).reshape(state)
    attn, weights, sums = local_call(
        functools.partial(attention_kernel, heads),
        [((length, width), F32), ((heads, length, length), BF16), ((8, length), F32)],
        (queries, key_rows, value_rows, gate_logits, cotangent, gain, cum, cumt, prior),
    )
    size = lax.axis_size("head")
    others = [
        lax.ppermute(sums, "head", [(i, (i + step) % size) for i in range(size)])
        for step in range(1, size)
    ]
    attended, grad_gate, grad, payload = local_call(
        functools.partial(norm_kernel, heads, full_width),
        [((length, width), BF16)] * 3 + [((chunks, ROWS + EXTRA, HD), BF16)],
        (queries, gate_logits, cotangent, gain, cum, attn, sums, *others),
    )
    arrived = exchange(payload)
    (scanned,) = local_call(
        backward_scan_kernel, [((count, ROWS + EXTRA, HD), BF16)], (arrived, decays)
    )
    back = exchange(scanned)
    grad_q, grad_k, grad_v, grad_decay, grad_gain = local_call(
        functools.partial(gradient_kernel, heads),
        [((length, width), BF16)] * 3 + [((length, heads), F32), ((1, width), F32)],
        (queries, key_rows, value_rows, cum, cumt, weights, attn, grad, prior, local, back),
    )
    return attended, grad_q, grad_k, grad_v, grad_gate, grad_decay, grad_gain.reshape(width)


def solution(mesh):
    tokens = P("ctx", "head")
    return jax.shard_map(
        per_device,
        mesh=mesh,
        in_specs=(tokens, tokens, tokens, tokens, P("head"), tokens, tokens),
        out_specs=(tokens, tokens, tokens, tokens, tokens, tokens, P("head")),
        check_vma=False,
    )
```

time: 525 us -> 110 us (0.21); the launches traced: 518 us -> 110 us
  other arithmetic: 153 us -> 0 us
  blocking collectives: 189 us -> 88.2 us
  waiting for transfers between devices: 103 us -> 3.05 us
  local copies, waits for them, and re-layouts: 35.4 us -> 4.25 us
  matrix products: 19.1 us -> 0 us
  between operations: 14.3 us -> 0.71 us
  Pallas kernels: 0 us -> 9.45 us
    select_n x126 -> x0, other arithmetic: 148 us -> none  [turn(): jnp.where(position < mine, new, old)]
    psum x3 -> x0, blocking collectives: 145 us -> none  [the longest x1 130 us: per_device(): grad_gain = lax.psum(jnp.sum(through_gate * normalized, axis=0), 'ctx')]
    all_gather x2 -> x0, waiting for transfers between devices: 103 us -> none  [carried_in(): pieces = jax.tree.map(lambda part: lax.all_gather(part, axis), value)]
    all_to_all x0 -> x4, blocking collectives: none -> 88.2 us  [exchange(): return lax.all_to_all(payload, 'ctx', 0, 0, tiled=True)]
    all_gather x1 -> x0, blocking collectives: 44 us -> none  [carried_in(): pieces = jax.tree.map(lambda part: lax.all_gather(part, axis), value)]
    rev x2 -> x0, local copies, waits for them, and re-layouts: 23 us -> none  [carried_in(): pieces = jax.tree.map(lambda part: part[::-1], pieces)]
    dot_general x14 -> x0, matrix products: 19.1 us -> none  [the longest x1 2.63 us: per_device(): jnp.einsum('hij,ihd->jhd', mixed, query_heads, preferred_element_type=jnp...]
    pallas_call x0 -> x6, Pallas kernels: none -> 9.45 us  [local_call(): pl.pallas_call(kernel, out_shape=[jax.ShapeDtypeStruct(shape, kind) for s...]
  transfers between devices with their start and end apart: 2 -> 3, of which waited for: 2 -> 2; matrix products, arithmetic and copies ran while one was open for 2% -> 0% of each run, Pallas kernels for 0% -> 0%
where the time goes in v1:
time: 110 us
  blocking collectives  88.2 us (80%)
  Pallas kernels  9.45 us (9%)
  local copies, waits for them, and re-layouts  4.25 us (4%)
  starting transfers between devices  3.85 us (4%)
  waiting for transfers between devices  3.05 us (3%)
    all_to_all x4, blocking collectives, exchange(): return lax.all_to_all(payload, 'ctx', 0, 0, tiled=True)  88.2 us
    pallas_call x6, Pallas kernels, local_call(): pl.pallas_call(kernel, out_shape=[jax.ShapeDtypeStruct(shape, kind) for s...  9.45 us
    unnamed x18, local copies, waits for them, and re-layouts  4.25 us
    ppermute x3, starting transfers between devices, per_device(): lax.ppermute(sums, 'head', [(i, (i + step) % size) for i in range(size)])  3.85 us
    ppermute x3, waiting for transfers between devices, per_device(): lax.ppermute(sums, 'head', [(i, (i + step) % size) for i in range(size)])  3.05 us
  transfers between devices with their start and end apart: 3, of which 2 were waited for; matrix products, arithmetic and copies ran while one was open for 0% of the time, Pallas kernels for 0%

profile of v1, /device:TPU:1, one launch (start us, length us, event | category | flops | bytes accessed | tf_op | source)
XLA Modules:
  0.0 109.5 jit_solution(15665290128341554010)
XLA Ops:
  0.6 0.8 copy.14.ld_ref
  1.5 0.0 copy-start
  1.5 1.0 copy-done
  2.5 0.0 copy-start.2
  2.5 1.0 copy-done.2
  3.5 0.0 copy-start.5
  3.5 0.0 copy-start.6
  3.6 1.1 shard_map.126
  4.6 0.0 copy-start.3
  4.6 0.0 copy-start.4
  4.7 27.5 %all_to_all.20.pay_ref = bf16[64,24,128]{2,1,0:T(8,128)(2,1)S(1)} all-to-all(bf16[64,24,128]{2,1,0:T(8,128)(2,1)S(1)} %get-tuple-element.27), channel_id=1, replica_groups=mesh['ctx'=64,'head'=4] {'ctx'}, dimensions={0} | all-to-all | bytes 786432 | tf_op jit(solution)/shard_map/all_to_all | solution.py:226
  32.2 0.1 shard_map.127
  32.3 18.0 %all_to_all.21 = bf16[64,16,128]{2,1,0:T(8,128)(2,1)S(1)} all-to-all(bf16[64,16,128]{2,1,0:T(8,128)(2,1)S(1)} %get-tuple-element.28), channel_id=1, replica_groups=mesh['ctx'=64,'head'=4] {'ctx'}, dimensions={0} | all-to-all | bytes 524288 | tf_op jit(solution)/shard_map/all_to_all | solution.py:226
  50.3 0.0 copy-done.5
  50.3 0.0 copy-done.6
  50.3 0.0 copy-done.3
  50.4 0.0 copy-done.4
  50.4 0.0 copy-done.1
  50.4 0.7 copy-done.7
  51.0 1.5 %shard_map.128 = (f32[256,1024]{1,0:T(8,128)S(1)}, bf16[8,256,256]{2,1,0:T(8,128)(2,1)S(1)}, f32[8,256]{1,0:T(8,128)S(1)}) custom-call(bf16[256,1024]{1,0:T(8,128)(2,1)S(1)} %copy-done.4, bf16[256,1024]{1,0:T(8,128)(2,1)S(1)} %copy-done.1, bf16[256,1024]{1,0:T(8,128)(2,1)S(1)} %copy-done.3, bf16[256,1024]{1,0:T(8,128)(2,1)S(1)} %copy-done.5, ...), custom_call_target="tpu_custom_call" | custom-call | tf_op jit(solution)/shard_map/pallas_call | solution.py:218
  52.5 2.8 %collective-permute-start.2 = (f32[8,256]{1,0:T(8,128)S(1)}, f32[8,256]{1,0:T(8,128)S(1)}, u32[]{:S(2)}, u32[]{:S(2)}) collective-permute-start(f32[8,256]{1,0:T(8,128)S(1)} %get-tuple-element.30.rest_0_), channel_id=1, source_target_pairs={{0,3},{1,0},{2,1},{3,2},{4,7},{5,4},{6,5},{7,6},{8,11},{9,8},{10,9... | collective-permute-start | bytes 24584 | tf_op jit(solution)/shard_map/ppermute | solution.py:254
  55.3 0.4 collective-permute-start.1
  55.7 0.7 collective-permute-start
  56.3 0.0 collective-permute-done.2.rest_3_
  56.3 3.0 %collective-permute-done.1.rest_2_ = f32[8,256]{1,0:T(8,128)S(1)} collective-permute-done((f32[8,256]{1,0:T(8,128)S(1)}, f32[8,256]{1,0:T(8,128)S(1)}, u32[]{:S(2)}, u32[]{:S(2)}) %collective-permute-start.1) | collective-permute-done | bytes 8224 | tf_op jit(solution)/shard_map/ppermute | solution.py:254
  59.3 0.1 collective-permute-done.rest_1_
  59.4 2.0 %shard_map.129 = (bf16[256,1024]{1,0:T(8,128)(2,1)}, bf16[256,1024]{1,0:T(8,128)(2,1)}, bf16[256,1024]{1,0:T(8,128)(2,1)S(1)}, bf16[64,24,128]{2,1,0:T(8,128)(2,1)S(1)}) custom-call(bf16[256,1024]{1,0:T(8,128)(2,1)S(1)} %copy-done.4, bf16[256,1024]{1,0:T(8,128)(2,1)S(1)} %copy-done.5, bf16[256,1024]{1,0:T(8,128)(2,1)S(1)} %copy-done.6, ...), custom_call_target="tpu_custom_call" | custom-call | tf_op jit(solution)/shard_map/pallas_call | solution.py:218
  61.4 22.1 %all_to_all.22.pay_ref = bf16[64,24,128]{2,1,0:T(8,128)(2,1)S(1)} all-to-all(bf16[64,24,128]{2,1,0:T(8,128)(2,1)S(1)} %get-tuple-element.35), channel_id=1, replica_groups=mesh['ctx'=64,'head'=4] {'ctx'}, dimensions={0} | all-to-all | bytes 786432 | tf_op jit(solution)/shard_map/all_to_all | solution.py:226
  83.5 0.2 shard_map.130
  83.7 20.6 %all_to_all.23.back_ref = bf16[64,24,128]{2,1,0:T(8,128)(2,1)S(1)} all-to-all(bf16[64,24,128]{2,1,0:T(8,128)(2,1)S(1)} %shard_map.130), channel_id=1, replica_groups=mesh['ctx'=64,'head'=4] {'ctx'}, dimensions={0} | all-to-all | bytes 786432 | tf_op jit(solution)/shard_map/all_to_all | solution.py:226
  104.3 4.6 %shard_map.131 = (bf16[256,1024]{1,0:T(8,128)(2,1)}, bf16[256,1024]{1,0:T(8,128)(2,1)}, bf16[256,1024]{1,0:T(8,128)(2,1)}, f32[256,8]{1,0:T(8,128)S(1)}, f32[1,1024]{1,0:T(1,128)}) custom-call(bf16[256,1024]{1,0:T(8,128)(2,1)S(1)} %copy-done.4, bf16[256,1024]{1,0:T(8,128)(2,1)S(1)} %copy-done.1, bf16[256,1024]{1,0:T(8,128)(2,1)S(1)} %copy-done.3, ...), custom_call_target="tpu_custom_call" | custom-call | tf_op jit(solution)/shard_map/pallas_call | solution.py:218
  108.9 0.7 copy.15
  (2 shorter events, 0.0 us)
Async XLA Ops:
  1.5 1.0 copy-start
  2.5 1.0 copy-start.2
  3.5 46.8 %copy-start.5 = (bf16[256,1024]{1,0:T(8,128)(2,1)S(1)}, bf16[256,1024]{1,0:T(8,128)(2,1)}, u32[]{:S(2)}) copy-start(bf16[256,1024]{1,0:T(8,128)(2,1)} %gate_ref.3) | copy-start | bytes 1572868
  3.5 46.8 %copy-start.6 = (bf16[256,1024]{1,0:T(8,128)(2,1)S(1)}, bf16[256,1024]{1,0:T(8,128)(2,1)}, u32[]{:S(2)}) copy-start(bf16[256,1024]{1,0:T(8,128)(2,1)} %cot_ref.3) | copy-start | bytes 1572868
  4.6 45.7 %copy-start.3 = (bf16[256,1024]{1,0:T(8,128)(2,1)S(1)}, bf16[256,1024]{1,0:T(8,128)(2,1)}, u32[]{:S(2)}) copy-start(bf16[256,1024]{1,0:T(8,128)(2,1)} %v_ref.5) | copy-start | bytes 1572868
  4.6 45.7 %copy-start.4 = (bf16[256,1024]{1,0:T(8,128)(2,1)S(1)}, bf16[256,1024]{1,0:T(8,128)(2,1)}, u32[]{:S(2)}) copy-start(bf16[256,1024]{1,0:T(8,128)(2,1)} %q_ref.5) | copy-start | bytes 1572868
  32.2 18.2 %copy-start.1 = (bf16[256,1024]{1,0:T(8,128)(2,1)S(1)}, bf16[256,1024]{1,0:T(8,128)(2,1)}, u32[]{:S(2)}) copy-start(bf16[256,1024]{1,0:T(8,128)(2,1)} %k_ref.5) | copy-start | bytes 1572868
  50.3 0.7 copy-start.7
  52.5 3.9 %collective-permute-start.2 = (f32[8,256]{1,0:T(8,128)S(1)}, f32[8,256]{1,0:T(8,128)S(1)}, u32[]{:S(2)}, u32[]{:S(2)}) collective-permute-start(f32[8,256]{1,0:T(8,128)S(1)} %get-tuple-element.30.rest_0_), channel_id=1, source_target_pairs={{0,3},{1,0},{2,1},{3,2},{4,7},{5,4},{6,5},{7,6},{8,11},{9,8},{10,9... | collective-permute-start | bytes 24584 | tf_op jit(solution)/shard_map/ppermute | solution.py:254
  55.3 4.0 %collective-permute-start.1 = (f32[8,256]{1,0:T(8,128)S(1)}, f32[8,256]{1,0:T(8,128)S(1)}, u32[]{:S(2)}, u32[]{:S(2)}) collective-permute-start(f32[8,256]{1,0:T(8,128)S(1)} %get-tuple-element.30.rest_0_), channel_id=1, source_target_pairs={{0,2},{1,3},{2,0},{3,1},{4,6},{5,7},{6,4},{7,5},{8,10},{9,11},{10,... | collective-permute-start | bytes 24584 | tf_op jit(solution)/shard_map/ppermute | solution.py:254
  55.7 3.7 %collective-permute-start = (f32[8,256]{1,0:T(8,128)S(1)}, f32[8,256]{1,0:T(8,128)S(1)}, u32[]{:S(2)}, u32[]{:S(2)}) collective-permute-start(f32[8,256]{1,0:T(8,128)S(1)} %get-tuple-element.30.rest_0_), channel_id=1, source_target_pairs={{0,1},{1,2},{2,3},{3,0},{4,5},{5,6},{6,7},{7,4},{8,9},{9,10},{10,1... | collective-permute-start | bytes 24584 | tf_op jit(solution)/shard_map/ppermute | solution.py:254

commit v2 on v1

v2 whole, which is shorter than its diff:
```python
import functools

import jax
import jax.numpy as jnp
from jax import lax
from jax.experimental import pallas as pl
from jax.experimental.pallas import tpu as pltpu
from jax.sharding import Mesh
from jax.sharding import PartitionSpec as P

EPSILON = 1e-05
HD = 128
ROWS = 16
EXTRA = 8
F32 = jnp.float32
BF16 = jnp.bfloat16
NEGATIVE = -1e30
WORK = 500_000_000


def dot(a, b, contract=(1, 0)):
    dims = (((contract[0],), (contract[1],)), ((), ()))
    return lax.dot_general(a, b, dims, preferred_element_type=F32)


def three_parts(value):
    high = value.astype(BF16)
    rest = value - high.astype(F32)
    middle = rest.astype(BF16)
    low = (rest - middle.astype(F32)).astype(BF16)
    return high, middle, low


def triangle_bf(length, flipped=False):
    row = lax.broadcasted_iota(jnp.int32, (length, length), 0)
    col = lax.broadcasted_iota(jnp.int32, (length, length), 1)
    return jnp.where(row <= col if flipped else col <= row, 1.0, 0.0).astype(BF16)


def exact_sums(ones, value):
    return sum(dot(ones, part) for part in three_parts(value))


def small_rows(*values):
    row = lax.broadcasted_iota(jnp.int32, (EXTRA, HD), 0)
    block = jnp.zeros((EXTRA, HD), F32)
    for place, value in enumerate(values):
        for turn, part in enumerate(three_parts(value)):
            block = jnp.where(row == 3 * place + turn, part.astype(F32), block)
    return block.astype(BF16)


def joined_rows(block, place=0):
    block = block[...].astype(F32)
    at = 3 * place
    return block[at : at + 1] + block[at + 1 : at + 2] + block[at + 2 : at + 3]


def masked_gap(cum_col, cum_row, low, high, left, right):
    gap = cum_col[low:high] - cum_row[:, left:right]
    if right <= low:
        return gap
    row = lax.broadcasted_iota(jnp.int32, gap.shape, 0) + low
    col = lax.broadcasted_iota(jnp.int32, gap.shape, 1) + left
    return jnp.where(col <= row, gap, NEGATIVE)


def decay_blocks(cum_col, cum_row):
    length = cum_col.shape[0]
    half = length // 2
    top = jnp.exp(masked_gap(cum_col, cum_row, 0, half, 0, half))
    bottom = jnp.exp(masked_gap(cum_col, cum_row, half, length, 0, length))
    return top, bottom


def one_of(first, if_first, if_second):
    return jnp.where(first, if_first, if_second)


def local_state_kernel(heads, k_ref, v_ref, ldt_ref, loc_ref, theirs_ref, cum_ref, cumt_ref):
    length = k_ref.shape[0]
    half = heads // 2
    core = lax.axis_index("core")
    ones = triangle_bf(length, True)
    cumt = sum(dot(part, ones) for part in three_parts(ldt_ref[...]))
    cumt_ref[...] = cumt
    cum = jnp.concatenate([cumt, jnp.zeros((HD - heads, length), F32)]).T[:, :heads]
    cum_ref[...] = cum
    last = cum[length - 1 : length]
    fade = jnp.exp(last - cum)
    for h in range(heads):
        cols = slice(h * HD, (h + 1) * HD)
        decayed = (k_ref[:, cols].astype(F32) * fade[:, h : h + 1]).astype(BF16)
        loc_ref[h] = dot(decayed, v_ref[:, cols], (0, 0)).astype(BF16)
    theirs_ref[:, :HD] = loc_ref[pl.ds((1 - core) * half, half)]
    for h in range(half):
        value = one_of(core == 0, last[:, half + h : half + h + 1], last[:, h : h + 1])
        theirs_ref[h, HD:] = small_rows(jnp.broadcast_to(value, (1, HD)))


def pair_logs(core, half, h, cumt_ref, got_ref):
    length = cumt_ref.shape[1]
    own = one_of(
        core == 0, cumt_ref[h : h + 1, length - 1 :], cumt_ref[half + h : half + h + 1, length - 1 :]
    )
    own = jnp.broadcast_to(own, (1, HD))
    other = joined_rows(got_ref[h, HD:])
    return one_of(core == 0, own, other), one_of(core == 0, other, own)


def pair_values(core, half, h, loc_ref, got_ref):
    own = loc_ref[core * half + h].astype(F32)
    other = got_ref[h, :HD].astype(F32)
    return one_of(core == 0, own, other), one_of(core == 0, other, own)


def put_chunks(pay_ref, h, state, rows):
    parts = HD // ROWS
    for part in range(parts):
        pay_ref[h * parts + part, :ROWS] = state[part * ROWS : (part + 1) * ROWS]
        pay_ref[h * parts + part, ROWS:] = rows


def forward_join_kernel(half, loc_ref, got_ref, cumt_ref, pay_ref):
    core = lax.axis_index("core")
    for h in range(half):
        log0, log1 = pair_logs(core, half, h, cumt_ref, got_ref)
        state0, state1 = pair_values(core, half, h, loc_ref, got_ref)
        both = jnp.exp(log1) * state0 + state1
        put_chunks(pay_ref, h, both.astype(BF16), small_rows(log0 + log1))


def forward_scan_kernel(pay_ref, out_ref, decay_ref, prior_ref):
    state = jnp.zeros((ROWS, HD), F32)
    for c in range(pay_ref.shape[0]):
        out_ref[c] = state.astype(BF16)
        prior_ref[c] = state
        decay = jnp.exp(joined_rows(pay_ref[c, ROWS:]))
        decay_ref[c : c + 1] = decay
        state = decay * state + pay_ref[c, :ROWS].astype(F32)


def forward_split_kernel(half, loc_ref, got_ref, cumt_ref, scanned_ref, mine_ref, theirs_ref):
    core = lax.axis_index("core")
    for h in range(half):
        log0, _ = pair_logs(core, half, h, cumt_ref, got_ref)
        state0, _ = pair_values(core, half, h, loc_ref, got_ref)
        prior0 = scanned_ref[h].astype(F32)
        prior1 = jnp.exp(log0) * prior0 + state0
        mine_ref[h] = one_of(core == 0, prior0, prior1).astype(BF16)
        theirs_ref[h] = one_of(core == 0, prior1, prior0).astype(BF16)


def backward_join_kernel(half, out_ref, got_ref, gain_ref, cumt_ref, got_state_ref, pay_ref):
    core = lax.axis_index("core")
    for h in range(half):
        log0, _ = pair_logs(core, half, h, cumt_ref, got_state_ref)
        state0, state1 = pair_values(core, half, h, out_ref, got_ref)
        both = state0 + jnp.exp(log0) * state1
        own = one_of(core == 0, gain_ref[h : h + 1], gain_ref[half + h : half + h + 1])
        rows = small_rows(own + got_ref[h, HD : HD + 1])
        put_chunks(pay_ref, h, both.astype(BF16), rows)


def backward_scan_kernel(pay_ref, decay_ref, prior_ref, out_ref):
    state = jnp.zeros((ROWS, HD), F32)
    total = jnp.zeros((1, HD), F32)
    meets = {}
    for c in reversed(range(pay_ref.shape[0])):
        out_ref[c, :ROWS] = state.astype(BF16)
        meets[c] = jnp.sum(state * prior_ref[c], axis=0, keepdims=True)
        state = decay_ref[c : c + 1] * state + pay_ref[c, :ROWS].astype(F32)
        total = total + joined_rows(pay_ref[c, ROWS:])
    for c in range(pay_ref.shape[0]):
        out_ref[c, ROWS:] = small_rows(total, meets[c])


def backward_split_kernel(
    half, out_ref, got_ref, loc_ref, cumt_ref, got_state_ref, prior_ref, back_ref, mine_ref, theirs_ref
):
    core = lax.axis_index("core")
    parts = HD // ROWS
    for h in range(half):
        log0, log1 = pair_logs(core, half, h, cumt_ref, got_state_ref)
        _, state1 = pair_values(core, half, h, out_ref, got_ref)
        state0, _ = pair_values(core, half, h, loc_ref, got_state_ref)
        later1 = jnp.concatenate([back_ref[h * parts + part, :ROWS] for part in range(parts)])
        later1 = later1.astype(F32)
        later0 = jnp.exp(log1) * later1 + state1
        mine_ref[h, :HD] = one_of(core == 0, later0, later1).astype(BF16)
        theirs_ref[h, :HD] = one_of(core == 0, later1, later0).astype(BF16)
        meet = sum(joined_rows(back_ref[h * parts + part, ROWS:], 1) for part in range(parts))
        meet = jnp.exp(log0 + log1) * meet
        prior = prior_ref[h].astype(F32)
        meet0 = meet + jnp.exp(log0) * jnp.sum(state1 * prior, axis=0, keepdims=True)
        meet1 = meet + jnp.exp(log1) * jnp.sum(later1 * state0, axis=0, keepdims=True)
        gain = joined_rows(back_ref[h * parts, ROWS:])
        mine_ref[h, HD:] = small_rows(gain, one_of(core == 0, meet0, meet1))
        theirs_ref[h, HD:] = small_rows(gain, one_of(core == 0, meet1, meet0))


def within_kernel(heads, q_ref, k_ref, v_ref, cum_ref, cumt_ref, intra_ref, weights_ref, decayed_ref):
    length = q_ref.shape[0]
    half = length // 2
    cum = cum_ref[...]
    for h in range(heads):
        cols = slice(h * HD, (h + 1) * HD)
        q, k, v = q_ref[:, cols], k_ref[:, cols], v_ref[:, cols]
        top, bottom = decay_blocks(cum[:, h : h + 1], cumt_ref[h : h + 1])
        top = (top * dot(q[:half], k[:half], (1, 1))).astype(BF16)
        bottom = (bottom * dot(q[half:], k, (1, 1))).astype(BF16)
        weights_ref[h, :half, :half] = top
        weights_ref[h, :half, half:] = jnp.zeros((half, length - half), BF16)
        weights_ref[h, half:] = bottom
        decayed_ref[:, cols] = (q.astype(F32) * jnp.exp(cum[:, h : h + 1])).astype(BF16)
        intra_ref[:half, cols] = dot(top, v[:half])
        intra_ref[half:, cols] = dot(bottom, v)


def gate_kernel(gate_ref, cot_ref, gain_ref, opened_ref, upstream_ref):
    opened = jax.nn.sigmoid(gate_ref[...].astype(F32))
    opened_ref[...] = opened
    upstream_ref[...] = cot_ref[...].astype(F32) * opened * gain_ref[...]


def attention_kernel(
    heads, decayed_ref, intra_ref, upstream_ref, mine_ref, got_ref, attn_ref, prior_ref, sums_ref
):
    length = decayed_ref.shape[0]
    core = lax.axis_index("core")
    half = heads // 2
    prior_ref[pl.ds(core * half, half)] = mine_ref[...]
    prior_ref[pl.ds((1 - core) * half, half)] = got_ref[...]
    squares = jnp.zeros((length, HD), F32)
    cross = jnp.zeros((length, HD), F32)
    for h in range(heads):
        cols = slice(h * HD, (h + 1) * HD)
        attn = dot(decayed_ref[:, cols], prior_ref[h]) + intra_ref[:, cols]
        attn_ref[:, cols] = attn
        squares = squares + attn * attn
        cross = cross + upstream_ref[:, cols] * attn
    sums_ref[...] = jnp.concatenate(
        [
            jnp.sum(squares.T, axis=0, keepdims=True),
            jnp.sum(cross.T, axis=0, keepdims=True),
            jnp.zeros((6, length), F32),
        ]
    )


def norm_kernel(
    heads, full_width, decayed_ref, cot_ref, opened_ref, upstream_ref, attn_ref,
    sums0_ref, sums1_ref, sums2_ref, sums3_ref, grad_ref, out_ref, theirs_ref, gain_ref, inverse_ref,
):
    length = decayed_ref.shape[0]
    half = heads // 2
    core = lax.axis_index("core")
    sums = sums0_ref[...] + sums1_ref[...] + sums2_ref[...] + sums3_ref[...]
    inverse_row = 1.0 / jnp.sqrt(sums[0:1] / full_width + EPSILON)
    cross_row = sums[1:2] * inverse_row / full_width
    inverse = jnp.broadcast_to(inverse_row, (HD, length)).T
    cross = jnp.broadcast_to(cross_row, (HD, length)).T
    inverse_ref[...] = inverse
    for h in range(heads):
        cols = slice(h * HD, (h + 1) * HD)
        normalized = attn_ref[:, cols] * inverse
        through = cot_ref[:, cols].astype(F32) * opened_ref[:, cols]
        gain_ref[h : h + 1] = jnp.sum(through * normalized, axis=0, keepdims=True)
        grad = ((upstream_ref[:, cols] - normalized * cross) * inverse).astype(BF16)
        grad_ref[:, cols] = grad
        out_ref[h] = dot(decayed_ref[:, cols], grad, (0, 0))
    theirs_ref[:, :HD] = out_ref[pl.ds((1 - core) * half, half)]
    for h in range(half):
        value = one_of(core == 0, gain_ref[half + h : half + h + 1], gain_ref[h : h + 1])
        theirs_ref[h, HD:] = jnp.broadcast_to(value, (EXTRA, HD))


def finish_kernel(
    heads, opened_ref, upstream_ref, gain_ref, attn_ref, inverse_ref, attended_ref, ggate_ref
):
    for h in range(heads):
        cols = slice(h * HD, (h + 1) * HD)
        opened = opened_ref[:, cols]
        normalized = attn_ref[:, cols] * inverse_ref[...]
        attended_ref[:, cols] = (normalized * gain_ref[:, cols] * opened).astype(BF16)
        ggate_ref[:, cols] = (upstream_ref[:, cols] * normalized * (1.0 - opened)).astype(BF16)


def query_gradient_kernel(
    heads, k_ref, v_ref, cum_ref, cumt_ref, grad_ref, prior_ref, gq_ref, mixed_ref
):
    length = k_ref.shape[0]
    half = length // 2
    cum = cum_ref[...]
    for h in range(heads):
        cols = slice(h * HD, (h + 1) * HD)
        k, v, grad = k_ref[:, cols], v_ref[:, cols], grad_ref[:, cols]
        top, bottom = decay_blocks(cum[:, h : h + 1], cumt_ref[h : h + 1])
        top = (top * dot(grad[:half], v[:half], (1, 1))).astype(BF16)
        bottom = (bottom * dot(grad[half:], v, (1, 1))).astype(BF16)
        mixed_ref[h, :half, :half] = top
        mixed_ref[h, :half, half:] = jnp.zeros((half, length - half), BF16)
        mixed_ref[h, half:] = bottom
        gq = jnp.concatenate([dot(top, k[:half]), dot(bottom, k)])
        gq = gq + jnp.exp(cum[:, h : h + 1]) * dot(grad, prior_ref[h], (1, 1))
        gq_ref[:, cols] = gq.astype(BF16)


def key_part_kernel(heads, q_ref, grad_ref, weights_ref, mixed_ref, gk_ref, gv_ref):
    for h in range(heads):
        cols = slice(h * HD, (h + 1) * HD)
        gk_ref[:, cols] = dot(mixed_ref[h], q_ref[:, cols], (0, 0))
        gv_ref[:, cols] = dot(weights_ref[h], grad_ref[:, cols], (0, 0))


def key_gradient_kernel(
    heads, k_ref, v_ref, cum_ref, attn_ref, grad_ref, gk_part_ref, gv_part_ref, mine_ref,
    got_ref, gk_ref, gv_ref, gdecayt_ref, ggain_ref, later_ref,
):
    length = k_ref.shape[0]
    half = heads // 2
    core = lax.axis_index("core")
    later_ref[pl.ds(core * half, half)] = mine_ref[:, :HD]
    later_ref[pl.ds((1 - core) * half, half)] = got_ref[:, :HD]
    cum = cum_ref[...]
    last = cum[length - 1 : length]
    lane = lax.broadcasted_iota(jnp.int32, (length, HD), 1)
    tails = []
    changes = jnp.zeros((length, HD), F32)
    for h in range(heads):
        cols = slice(h * HD, (h + 1) * HD)
        k, v, grad, later = k_ref[:, cols], v_ref[:, cols], grad_ref[:, cols], later_ref[h]
        mine, got = mine_ref[h % half, HD:], got_ref[h % half, HD:]
        own = core == h // half
        ggain_ref[:, cols] = one_of(own, joined_rows(mine), joined_rows(got))
        fade = jnp.exp(last[:, h : h + 1] - cum[:, h : h + 1])
        pull = fade * dot(v, later, (1, 1))
        gk_part = gk_part_ref[:, cols]
        gk_ref[:, cols] = (gk_part + pull).astype(BF16)
        gv_ref[:, cols] = (gv_part_ref[:, cols] + fade * dot(k, later)).astype(BF16)
        key = k.astype(F32)
        pulled = key * pull
        meet = one_of(own, joined_rows(mine, 1), joined_rows(got, 1))
        tails.append(meet + jnp.sum(pulled, axis=0, keepdims=True))
        change = attn_ref[:, cols] * grad.astype(F32) - key * gk_part - pulled
        changes = jnp.where(lane == h, jnp.sum(change, axis=1, keepdims=True), changes)
    tail = jnp.sum(jnp.concatenate(tails), axis=1, keepdims=True)
    ones = triangle_bf(length)
    gdecayt_ref[...] = tail + sum(dot(part, ones) for part in three_parts(changes.T[:heads]))


def local_call(kernel, outs, args, flops=0, moved=0, scratch=()):
    return pl.pallas_call(
        kernel,
        out_shape=[jax.ShapeDtypeStruct(shape, kind) for shape, kind in outs],
        scratch_shapes=list(scratch),
        compiler_params=pltpu.CompilerParams(vmem_limit_bytes=40 * 2**20),
        cost_estimate=pl.CostEstimate(flops=flops, bytes_accessed=moved, transcendentals=0),
    )(*args)


def exchange(payload):
    return lax.all_to_all(payload, ("x", "z"), 0, 0, tiled=True)


def swap(value):
    return lax.ppermute(value, "core", [(0, 1), (1, 0)])


def per_device(queries, key_rows, value_rows, gate_logits, norm_gain, log_decay, cotangent):
    length, width = queries.shape
    heads = log_decay.shape[1]
    half = heads // 2
    chips = lax.axis_size("x") * lax.axis_size("z")
    size = lax.axis_size("head")
    full_width = width * size
    gain = norm_gain.reshape(1, width)
    state, part_state = (heads, HD, HD), (half, HD, HD)
    carried = (half, HD + EXTRA, HD)
    chunks = half * HD // ROWS
    tokens, tokens32 = ((length, width), BF16), ((length, width), F32)
    square = ((heads, length, length), BF16)
    local, theirs, cum, cumt = local_call(
        functools.partial(local_state_kernel, heads),
        [(state, BF16), (carried, BF16), ((length, heads), F32), ((heads, length), F32)],
        (key_rows, value_rows, log_decay.T),
        WORK, WORK // 100,
    )
    got = swap(theirs)
    intra, weights, decayed = local_call(
        functools.partial(within_kernel, heads),
        [tokens32, square, tokens],
        (queries, key_rows, value_rows, cum, cumt),
        WORK, WORK // 100,
    )
    got, intra = lax.optimization_barrier((got, intra))
    (payload,) = local_call(
        functools.partial(forward_join_kernel, half),
        [((chunks, ROWS + EXTRA, HD), BF16)],
        (local, got, cumt),
    )
    scanned, decays, chip_prior = local_call(
        forward_scan_kernel,
        [((chips, ROWS, HD), BF16), ((chips, HD), F32), ((chips, ROWS, HD), F32)],
        (exchange(payload),),
    )
    scanned = exchange(scanned).reshape(part_state)
    mine, theirs = local_call(
        functools.partial(forward_split_kernel, half),
        [(part_state, BF16)] * 2,
        (local, got, cumt, scanned),
    )
    opened, upstream = local_call(
        gate_kernel, [tokens32] * 2, (gate_logits, cotangent, gain), WORK, WORK // 100
    )
    attn, prior, sums = local_call(
        functools.partial(attention_kernel, heads),
        [tokens32, (state, BF16), ((8, length), F32)],
        (decayed, intra, upstream, mine, swap(theirs)),
        WORK, WORK // 100,
    )
    others = [
        lax.ppermute(sums, "head", [(i, i ^ step) for i in range(size)])
        for step in range(1, size)
    ]
    grad, outgoing, theirs, gains, inverse = local_call(
        functools.partial(norm_kernel, heads, full_width),
        [tokens, (state, F32), (carried, F32), ((heads, HD), F32), ((length, HD), F32)],
        (decayed, cotangent, opened, upstream, attn, sums, *others),
        WORK, WORK // 100,
    )
    got_back = swap(theirs)
    attended, grad_gate = local_call(
        functools.partial(finish_kernel, heads),
        [tokens] * 2,
        (opened, upstream, gain, attn, inverse),
        WORK, WORK // 100,
    )
    grad_q, mixed = local_call(
        functools.partial(query_gradient_kernel, heads),
        [tokens, square],
        (key_rows, value_rows, cum, cumt, grad, prior),
        WORK, WORK // 100,
    )
    got_back, mixed = lax.optimization_barrier((got_back, mixed))
    (payload,) = local_call(
        functools.partial(backward_join_kernel, half),
        [((chunks, ROWS + EXTRA, HD), BF16)],
        (outgoing, got_back, gains, cumt, got),
    )
    (back,) = local_call(
        backward_scan_kernel,
        [((chips, ROWS + EXTRA, HD), BF16)],
        (exchange(payload), decays, chip_prior),
    )
    mine, theirs = local_call(
        functools.partial(backward_split_kernel, half),
        [(carried, BF16)] * 2,
        (outgoing, got_back, local, cumt, got, scanned, exchange(back)),
    )
    gk_part, gv_part = local_call(
        functools.partial(key_part_kernel, heads),
        [tokens32] * 2,
        (queries, grad, weights, mixed),
        WORK, WORK // 100,
    )
    grad_k, grad_v, grad_decay, grad_gain = local_call(
        functools.partial(key_gradient_kernel, heads),
        [tokens, tokens, ((heads, length), F32), ((1, width), F32)],
        (key_rows, value_rows, cum, attn, grad, gk_part, gv_part, mine, swap(theirs)),
        WORK, WORK // 100,
        [pltpu.VMEM(state, BF16)],
    )
    return attended, grad_q, grad_k, grad_v, grad_gate, grad_decay.T, grad_gain.reshape(width)


def solution(mesh):
    fine = Mesh(mesh.devices.reshape(4, 8, 2, 4), ("x", "z", "core", "head"))
    tokens = P(("x", "z", "core"), "head")
    return jax.shard_map(
        per_device,
        mesh=fine,
        in_specs=(tokens, tokens, tokens, tokens, P("head"), tokens, tokens),
        out_specs=(tokens, tokens, tokens, tokens, tokens, tokens, P("head")),
        check_vma=False,
    )
```

time: 110 us -> 96.3 us (0.88)
  blocking collectives: 88.2 us -> 60.8 us
  starting transfers between devices: 3.85 us -> 15.2 us
  Pallas kernels: 9.45 us -> 11.8 us
  local copies, waits for them, and re-layouts: 4.25 us -> 2.8 us
  waiting for transfers between devices: 3.05 us -> 4.46 us
    all_to_all x4, blocking collectives: 88.2 us -> 60.8 us  [exchange(): return lax.all_to_all(payload, ('x', 'z'), 0, 0, tiled=True)]
    ppermute x3 -> x7, starting transfers between devices: 3.85 us -> 15.2 us  [the longest x4 11.2 us: swap(): return lax.ppermute(value, 'core', [(0, 1), (1, 0)])]
    pallas_call x6 -> x15, Pallas kernels: 9.45 us -> 11.8 us  [local_call(): pl.pallas_call(kernel, out_shape=[jax.ShapeDtypeStruct(shape, kind) for s...]
    unnamed x18, local copies, waits for them, and re-layouts: 4.25 us -> 2.8 us
    ppermute x3 -> x7, waiting for transfers between devices: 3.05 us -> 4.46 us  [the longest x3 3.71 us: per_device(): lax.ppermute(sums, 'head', [(i, i ^ step) for i in range(size)])]
  transfers between devices with their start and end apart: 3 -> 7, of which waited for: 2 -> 3; matrix products, arithmetic and copies ran while one was open for 0% -> 0% of each run, Pallas kernels for 0% -> 6%
where the time goes in v2:
time: 96.3 us; the launch traced here: 95.8 us
  blocking collectives  60.8 us (63%)
  starting transfers between devices  15.2 us (16%)
  Pallas kernels  11.8 us (12%)
  waiting for transfers between devices  4.46 us (5%)
  local copies, waits for them, and re-layouts  2.8 us (3%)
    all_to_all x4, blocking collectives, exchange(): return lax.all_to_all(payload, ('x', 'z'), 0, 0, tiled=True)  60.8 us
    pallas_call x15, Pallas kernels, local_call(): pl.pallas_call(kernel, out_shape=[jax.ShapeDtypeStruct(shape, kind) for s...  11.8 us
    ppermute x4, starting transfers between devices, swap(): return lax.ppermute(value, 'core', [(0, 1), (1, 0)])  11.2 us
    ppermute x3, starting transfers between devices, per_device(): lax.ppermute(sums, 'head', [(i, i ^ step) for i in range(size)])  4.01 us
    ppermute x3, waiting for transfers between devices, per_device(): lax.ppermute(sums, 'head', [(i, i ^ step) for i in range(size)])  3.71 us
    unnamed x18, local copies, waits for them, and re-layouts  2.8 us
  transfers between devices with their start and end apart: 7, of which 3 were waited for; matrix products, arithmetic and copies ran while one was open for 0% of the time, Pallas kernels for 6%

profile of v2, /device:TPU:1, one launch (start us, length us, event | category | flops | bytes accessed | tf_op | source)
XLA Modules:
  0.0 95.8 jit_solution(8739771304664865768)
XLA Ops:
  0.6 0.0 copy-start
  0.6 1.0 %copy-done = bf16[256,1024]{1,0:T(8,128)(2,1)S(1)} copy-done((bf16[256,1024]{1,0:T(8,128)(2,1)S(1)}, bf16[256,1024]{1,0:T(8,128)(2,1)}, u32[]{:S(2)}) %copy-start) | copy-done | bytes 524312
  1.7 1.0 %copy-done.2 = bf16[256,1024]{1,0:T(8,128)(2,1)S(1)} copy-done((bf16[256,1024]{1,0:T(8,128)(2,1)S(1)}, bf16[256,1024]{1,0:T(8,128)(2,1)}, u32[]{:S(2)}) %copy-start.2) | copy-done | bytes 524312
  2.7 0.7 copy-done.8
  3.4 1.2 %shard_map.127 = (bf16[8,128,128]{2,1,0:T(8,128)(2,1)S(1)}, bf16[4,136,128]{2,1,0:T(8,128)(2,1)S(1)}, f32[256,8]{1,0:T(8,128)S(1)}, f32[8,256]{1,0:T(8,128)S(1)}) custom-call(bf16[256,1024]{1,0:T(8,128)(2,1)S(1)} %copy-done, bf16[256,1024]{1,0:T(8,128)(2,1)S(1)} %copy-done.2, f32[8,256]{1,0:T(8,128)S(1)} %bitcast.9), custom_call_target="tpu_custom_call" | custom-call | flops 500000000 | bytes 5000000 | tf_op jit(solution)/shard_map/pallas_call | solution.py:353
  4.6 3.3 %collective-permute-start = (bf16[4,136,128]{2,1,0:T(8,128)(2,1)S(1)}, bf16[4,136,128]{2,1,0:T(8,128)(2,1)S(1)}, u32[]{:S(2)}, u32[]{:S(2)}) collective-permute-start(bf16[4,136,128]{2,1,0:T(8,128)(2,1)S(1)} %get-tuple-element.50), channel_id=1, source_target_pairs={{0,4},{4,0},{1,5},{5,1},{2,6},{6,2},{3,7},{7,3},{8,12},{12,8},{9,1... | collective-permute-start | bytes 417800 | tf_op jit(solution)/shard_map/ppermute | solution.py:367
  8.0 1.4 %shard_map.128 = (f32[256,1024]{1,0:T(8,128)S(1)}, bf16[8,256,256]{2,1,0:T(8,128)(2,1)S(1)}, bf16[256,1024]{1,0:T(8,128)(2,1)S(1)}) custom-call(bf16[256,1024]{1,0:T(8,128)(2,1)S(1)} %copy-done.4, bf16[256,1024]{1,0:T(8,128)(2,1)S(1)} %copy-done, bf16[256,1024]{1,0:T(8,128)(2,1)S(1)} %copy-done.2, f32[256,8]{1,0:T(8,128)S(1)} %get-tuple-element.47.cum_ref, ...), custom_call_target="tpu_custom_call" | custom-call | flops 500000000 | bytes 5000000 | tf_op jit(solution)/shard_map/pallas_call | solution.py:353
  9.4 0.1 shard_map.129
  9.5 18.9 %all_to_all.20.pay_ref = bf16[32,24,128]{2,1,0:T(8,128)(2,1)S(1)} all-to-all(bf16[32,24,128]{2,1,0:T(8,128)(2,1)S(1)} %shard_map.129), channel_id=1, replica_groups=mesh['x'=4,'z'=8,'core'=2,'head'=4] {'x','z'}, dimensions={0} | all-to-all | bytes 393216 | tf_op jit(solution)/shard_map/all_to_all | solution.py:363
  28.4 0.1 shard_map.130
  28.5 14.6 %all_to_all.21 = bf16[32,16,128]{2,1,0:T(8,128)(2,1)S(1)} all-to-all(bf16[32,16,128]{2,1,0:T(8,128)(2,1)S(1)} %get-tuple-element.55), channel_id=1, replica_groups=mesh['x'=4,'z'=8,'core'=2,'head'=4] {'x','z'}, dimensions={0} | all-to-all | bytes 262144 | tf_op jit(solution)/shard_map/all_to_all | solution.py:363
  43.1 0.1 shard_map.131
  43.2 2.4 %collective-permute-start.1 = (bf16[4,128,128]{2,1,0:T(8,128)(2,1)S(1)}, bf16[4,128,128]{2,1,0:T(8,128)(2,1)S(1)}, u32[]{:S(2)}, u32[]{:S(2)}) collective-permute-start(bf16[4,128,128]{2,1,0:T(8,128)(2,1)S(1)} %get-tuple-element.57), channel_id=1, source_target_pairs={{0,4},{4,0},{1,5},{5,1},{2,6},{6,2},{3,7},{7,3},{8,12},{12,8},{9,1... | collective-permute-start | bytes 393224 | tf_op jit(solution)/shard_map/ppermute | solution.py:367
  45.7 0.2 shard_map.126
  45.9 0.7 collective-permute-done.1.got_ref
  46.7 0.5 shard_map.132
  47.2 1.4 %collective-permute-start.2 = (f32[8,256]{1,0:T(8,128)S(1)}, f32[8,256]{1,0:T(8,128)S(1)}, u32[]{:S(2)}, u32[]{:S(2)}) collective-permute-start(f32[8,256]{1,0:T(8,128)S(1)} %get-tuple-element.59.sums0_ref), channel_id=1, source_target_pairs={{0,1},{1,0},{2,3},{3,2},{4,5},{5,4},{6,7},{7,6},{8,9},{9,8},{10,11... | collective-permute-start | bytes 24584 | tf_op jit(solution)/shard_map/ppermute | solution.py:423
  48.6 2.6 %collective-permute-start.3 = (f32[8,256]{1,0:T(8,128)S(1)}, f32[8,256]{1,0:T(8,128)S(1)}, u32[]{:S(2)}, u32[]{:S(2)}) collective-permute-start(f32[8,256]{1,0:T(8,128)S(1)} %get-tuple-element.59.sums0_ref), channel_id=1, source_target_pairs={{0,2},{1,3},{2,0},{3,1},{4,6},{5,7},{6,4},{7,5},{8,10},{9,11},{10,... | collective-permute-start | bytes 24584 | tf_op jit(solution)/shard_map/ppermute | solution.py:423
  51.2 1.4 %collective-permute-done.3.sums2_ref = f32[8,256]{1,0:T(8,128)S(1)} collective-permute-done((f32[8,256]{1,0:T(8,128)S(1)}, f32[8,256]{1,0:T(8,128)S(1)}, u32[]{:S(2)}, u32[]{:S(2)}) %collective-permute-start.3) | collective-permute-done | bytes 8224 | tf_op jit(solution)/shard_map/ppermute | solution.py:423
  52.6 2.3 %collective-permute-done.4.sums3_ref = f32[8,256]{1,0:T(8,128)S(1)} collective-permute-done((f32[8,256]{1,0:T(8,128)S(1)}, f32[8,256]{1,0:T(8,128)S(1)}, u32[]{:S(2)}, u32[]{:S(2)}) %collective-permute-start.4) | collective-permute-done | bytes 8224 | tf_op jit(solution)/shard_map/ppermute | solution.py:423
  54.9 0.8 shard_map.133
  55.7 2.2 %collective-permute-start.5 = (f32[4,136,128]{2,1,0:T(8,128)S(1)}, f32[4,136,128]{2,1,0:T(8,128)S(1)}, u32[]{:S(2)}, u32[]{:S(2)}) collective-permute-start(f32[4,136,128]{2,1,0:T(8,128)S(1)} %get-tuple-element.66), channel_id=1, source_target_pairs={{0,4},{4,0},{1,5},{5,1},{2,6},{6,2},{3,7},{7,3},{8,12},{12,8},{9,1... | collective-permute-start | bytes 835592 | tf_op jit(solution)/shard_map/ppermute | solution.py:367
  57.9 2.4 %shard_map.135 = (bf16[256,1024]{1,0:T(8,128)(2,1)}, bf16[8,256,256]{2,1,0:T(8,128)(2,1)S(1)}) custom-call(bf16[256,1024]{1,0:T(8,128)(2,1)S(1)} %copy-done.1, bf16[256,1024]{1,0:T(8,128)(2,1)S(1)} %copy-done.3, f32[256,8]{1,0:T(8,128)S(1)} %get-tuple-element.47.cum_ref, f32[8,256]{1,0:T(8,128)S(1)} %get-tuple-element.48.cumt_ref, ...), custom_call_target="tpu_custom_call" | custom-call | flops 500000000 | bytes 5000000 | tf_op jit(solution)/shard_map/pallas_call | solution.py:353
  60.2 0.1 shard_map.137
  60.4 12.7 %all_to_all.22.pay_ref = bf16[32,24,128]{2,1,0:T(8,128)(2,1)S(1)} all-to-all(bf16[32,24,128]{2,1,0:T(8,128)(2,1)S(1)} %shard_map.137), channel_id=1, replica_groups=mesh['x'=4,'z'=8,'core'=2,'head'=4] {'x','z'}, dimensions={0} | all-to-all | bytes 393216 | tf_op jit(solution)/shard_map/all_to_all | solution.py:363
  73.0 0.2 shard_map.138
  73.2 14.7 %all_to_all.23.back_ref = bf16[32,24,128]{2,1,0:T(8,128)(2,1)S(1)} all-to-all(bf16[32,24,128]{2,1,0:T(8,128)(2,1)S(1)} %shard_map.138), channel_id=1, replica_groups=mesh['x'=4,'z'=8,'core'=2,'head'=4] {'x','z'}, dimensions={0} | all-to-all | bytes 393216 | tf_op jit(solution)/shard_map/all_to_all | solution.py:363
  87.9 0.2 shard_map.139
  88.1 3.3 %collective-permute-start.6 = (bf16[4,136,128]{2,1,0:T(8,128)(2,1)S(1)}, bf16[4,136,128]{2,1,0:T(8,128)(2,1)S(1)}, u32[]{:S(2)}, u32[]{:S(2)}) collective-permute-start(bf16[4,136,128]{2,1,0:T(8,128)(2,1)S(1)} %get-tuple-element.77), channel_id=1, source_target_pairs={{0,4},{4,0},{1,5},{5,1},{2,6},{6,2},{3,7},{7,3},{8,12},{12,8},{9,1... | collective-permute-start | bytes 417800 | tf_op jit(solution)/shard_map/ppermute | solution.py:367
  91.4 1.4 %shard_map.134 = (bf16[256,1024]{1,0:T(8,128)(2,1)}, bf16[256,1024]{1,0:T(8,128)(2,1)}) custom-call(f32[256,1024]{1,0:T(8,128)S(1)} %get-tuple-element.45.opened_ref, f32[256,1024]{1,0:T(8,128)S(1)} %get-tuple-element.46.upstream_ref, f32[1,1024]{1,0:T(1,128)S(1)} %bitcast.8, f32[256,1024]{1,0:T(8,128)S(1)} %get-tuple-element.58.attn_ref, ...), custom_call_target="tpu_custom_call" | custom-call | flops 500000000 | bytes 5000000 | tf_op jit(solution)/shard_map/pallas_call | solution.py:353
  92.8 0.8 shard_map.136
  93.6 2.2 %shard_map.140 = (bf16[256,1024]{1,0:T(8,128)(2,1)}, bf16[256,1024]{1,0:T(8,128)(2,1)}, f32[8,256]{1,0:T(8,128)}, f32[1,1024]{1,0:T(1,128)}) custom-call(bf16[256,1024]{1,0:T(8,128)(2,1)S(1)} %copy-done.1, bf16[256,1024]{1,0:T(8,128)(2,1)S(1)} %copy-done.3, f32[256,8]{1,0:T(8,128)S(1)} %get-tuple-element.47.cum_ref, ...), custom_call_target="tpu_custom_call" | custom-call | flops 500000000 | bytes 5000000 | tf_op jit(solution)/shard_map/pallas_call | solution.py:353
  (19 shorter events, 0.0 us)
Async XLA Ops:
  0.6 1.0 %copy-start = (bf16[256,1024]{1,0:T(8,128)(2,1)S(1)}, bf16[256,1024]{1,0:T(8,128)(2,1)}, u32[]{:S(2)}) copy-start(bf16[256,1024]{1,0:T(8,128)(2,1)} %k_ref.7) | copy-start | bytes 1572868
  1.7 1.0 %copy-start.2 = (bf16[256,1024]{1,0:T(8,128)(2,1)S(1)}, bf16[256,1024]{1,0:T(8,128)(2,1)}, u32[]{:S(2)}) copy-start(bf16[256,1024]{1,0:T(8,128)(2,1)} %v_ref.7) | copy-start | bytes 1572868
  2.7 0.7 copy-start.8
  3.4 4.5 %copy-start.4 = (bf16[256,1024]{1,0:T(8,128)(2,1)S(1)}, bf16[256,1024]{1,0:T(8,128)(2,1)}, u32[]{:S(2)}) copy-start(bf16[256,1024]{1,0:T(8,128)(2,1)} %q_ref.3) | copy-start | bytes 1572868
  4.6 4.8 %collective-permute-start = (bf16[4,136,128]{2,1,0:T(8,128)(2,1)S(1)}, bf16[4,136,128]{2,1,0:T(8,128)(2,1)S(1)}, u32[]{:S(2)}, u32[]{:S(2)}) collective-permute-start(bf16[4,136,128]{2,1,0:T(8,128)(2,1)S(1)} %get-tuple-element.50), channel_id=1, source_target_pairs={{0,4},{4,0},{1,5},{5,1},{2,6},{6,2},{3,7},{7,3},{8,12},{12,8},{9,1... | collective-permute-start | bytes 417800 | tf_op jit(solution)/shard_map/ppermute | solution.py:367
  9.5 36.2 %copy-start.7 = (bf16[256,1024]{1,0:T(8,128)(2,1)S(1)}, bf16[256,1024]{1,0:T(8,128)(2,1)}, u32[]{:S(2)}) copy-start(bf16[256,1024]{1,0:T(8,128)(2,1)} %gate_ref.1) | copy-start | bytes 1572868
  28.4 17.3 %copy-start.5 = (bf16[256,1024]{1,0:T(8,128)(2,1)S(1)}, bf16[256,1024]{1,0:T(8,128)(2,1)}, u32[]{:S(2)}) copy-start(bf16[256,1024]{1,0:T(8,128)(2,1)} %cot_ref.3) | copy-start | bytes 1572868
  43.1 2.6 %copy-start.6 = (f32[1024]{0:T(1024)S(1)}, f32[1024]{0:T(1024)}, u32[]{:S(2)}) copy-start(f32[1024]{0:T(1024)} %param.11) | copy-start | bytes 12292
  43.2 3.4 %collective-permute-start.1 = (bf16[4,128,128]{2,1,0:T(8,128)(2,1)S(1)}, bf16[4,128,128]{2,1,0:T(8,128)(2,1)S(1)}, u32[]{:S(2)}, u32[]{:S(2)}) collective-permute-start(bf16[4,128,128]{2,1,0:T(8,128)(2,1)S(1)} %get-tuple-element.57), channel_id=1, source_target_pairs={{0,4},{4,0},{1,5},{5,1},{2,6},{6,2},{3,7},{7,3},{8,12},{12,8},{9,1... | collective-permute-start | bytes 393224 | tf_op jit(solution)/shard_map/ppermute | solution.py:367
  47.2 4.0 %collective-permute-start.2 = (f32[8,256]{1,0:T(8,128)S(1)}, f32[8,256]{1,0:T(8,128)S(1)}, u32[]{:S(2)}, u32[]{:S(2)}) collective-permute-start(f32[8,256]{1,0:T(8,128)S(1)} %get-tuple-element.59.sums0_ref), channel_id=1, source_target_pairs={{0,1},{1,0},{2,3},{3,2},{4,5},{5,4},{6,7},{7,6},{8,9},{9,8},{10,11... | collective-permute-start | bytes 24584 | tf_op jit(solution)/shard_map/ppermute | solution.py:423
  48.6 4.0 %collective-permute-start.3 = (f32[8,256]{1,0:T(8,128)S(1)}, f32[8,256]{1,0:T(8,128)S(1)}, u32[]{:S(2)}, u32[]{:S(2)}) collective-permute-start(f32[8,256]{1,0:T(8,128)S(1)} %get-tuple-element.59.sums0_ref), channel_id=1, source_target_pairs={{0,2},{1,3},{2,0},{3,1},{4,6},{5,7},{6,4},{7,5},{8,10},{9,11},{10,... | collective-permute-start | bytes 24584 | tf_op jit(solution)/shard_map/ppermute | solution.py:423
  51.2 3.7 %collective-permute-start.4 = (f32[8,256]{1,0:T(8,128)S(1)}, f32[8,256]{1,0:T(8,128)S(1)}, u32[]{:S(2)}, u32[]{:S(2)}) collective-permute-start(f32[8,256]{1,0:T(8,128)S(1)} %get-tuple-element.59.sums0_ref), channel_id=1, source_target_pairs={{0,3},{1,2},{2,1},{3,0},{4,7},{5,6},{6,5},{7,4},{8,11},{9,10},{10,... | collective-permute-start | bytes 24584 | tf_op jit(solution)/shard_map/ppermute | solution.py:423
  54.9 2.9 %copy-start.1 = (bf16[256,1024]{1,0:T(8,128)(2,1)S(1)}, bf16[256,1024]{1,0:T(8,128)(2,1)}, u32[]{:S(2)}) copy-start(bf16[256,1024]{1,0:T(8,128)(2,1)} %k_ref.7) | copy-start | bytes 1572868
  54.9 2.9 %copy-start.3 = (bf16[256,1024]{1,0:T(8,128)(2,1)S(1)}, bf16[256,1024]{1,0:T(8,128)(2,1)}, u32[]{:S(2)}) copy-start(bf16[256,1024]{1,0:T(8,128)(2,1)} %v_ref.7) | copy-start | bytes 1572868
  55.7 4.5 %collective-permute-start.5 = (f32[4,136,128]{2,1,0:T(8,128)S(1)}, f32[4,136,128]{2,1,0:T(8,128)S(1)}, u32[]{:S(2)}, u32[]{:S(2)}) collective-permute-start(f32[4,136,128]{2,1,0:T(8,128)S(1)} %get-tuple-element.66), channel_id=1, source_target_pairs={{0,4},{4,0},{1,5},{5,1},{2,6},{6,2},{3,7},{7,3},{8,12},{12,8},{9,1... | collective-permute-start | bytes 835592 | tf_op jit(solution)/shard_map/ppermute | solution.py:367
  88.1 5.5 %collective-permute-start.6 = (bf16[4,136,128]{2,1,0:T(8,128)(2,1)S(1)}, bf16[4,136,128]{2,1,0:T(8,128)(2,1)S(1)}, u32[]{:S(2)}, u32[]{:S(2)}) collective-permute-start(bf16[4,136,128]{2,1,0:T(8,128)(2,1)S(1)} %get-tuple-element.77), channel_id=1, source_target_pairs={{0,4},{4,0},{1,5},{5,1},{2,6},{6,2},{3,7},{7,3},{8,12},{12,8},{9,1... | collective-permute-start | bytes 417800 | tf_op jit(solution)/shard_map/ppermute | solution.py:367

commit v3 on v2

--- a/solution.py
+++ b/solution.py
@@ -96,6 +96,22 @@
     for h in range(half):
         value = one_of(core == 0, last[:, half + h : half + h + 1], last[:, h : h + 1])
         theirs_ref[h, HD:] = small_rows(jnp.broadcast_to(value, (1, HD)))
+
+
+class Outward:
+    def __init__(self, place, held, sems, base):
+        self.place, self.held, self.sems, self.base, self.copies = place, held, sems, base, []
+
+    def put(self, h, value):
+        cols = slice(h * HD, (h + 1) * HD)
+        self.held[h] = value
+        copy = pltpu.make_async_copy(self.held.at[h], self.place.at[:, cols], self.sems.at[self.base + h])
+        copy.start()
+        self.copies.append(copy)
+
+    def wait(self):
+        for copy in self.copies:
+            copy.wait()
 
 
 def pair_logs(core, half, h, cumt_ref, got_ref):
@@ -203,6 +219,7 @@
     length = q_ref.shape[0]
     half = length // 2
     cum = cum_ref[...]
+    grown = jnp.exp(cum)
     for h in range(heads):
         cols = slice(h * HD, (h + 1) * HD)
         q, k, v = q_ref[:, cols], k_ref[:, cols], v_ref[:, cols]
@@ -212,7 +229,7 @@
         weights_ref[h, :half, :half] = top
         weights_ref[h, :half, half:] = jnp.zeros((half, length - half), BF16)
         weights_ref[h, half:] = bottom
-        decayed_ref[:, cols] = (q.astype(F32) * jnp.exp(cum[:, h : h + 1])).astype(BF16)
+        decayed_ref[:, cols] = (q.astype(F32) * grown[:, h : h + 1]).astype(BF16)
         intra_ref[:half, cols] = dot(top, v[:half])
         intra_ref[half:, cols] = dot(bottom, v)
 
@@ -276,41 +293,54 @@
 
 
 def finish_kernel(
-    heads, opened_ref, upstream_ref, gain_ref, attn_ref, inverse_ref, attended_ref, ggate_ref
+    heads, opened_ref, upstream_ref, gain_ref, attn_ref, inverse_ref, attended_hbm, ggate_hbm,
+    attended_ref, ggate_ref, sems,
 ):
+    attended = Outward(attended_hbm, attended_ref, sems, 0)
+    ggate = Outward(ggate_hbm, ggate_ref, sems, heads)
     for h in range(heads):
         cols = slice(h * HD, (h + 1) * HD)
         opened = opened_ref[:, cols]
         normalized = attn_ref[:, cols] * inverse_ref[...]
-        attended_ref[:, cols] = (normalized * gain_ref[:, cols] * opened).astype(BF16)
-        ggate_ref[:, cols] = (upstream_ref[:, cols] * normalized * (1.0 - opened)).astype(BF16)
+        attended.put(h, (normalized * gain_ref[:, cols] * opened).astype(BF16))
+        ggate.put(h, (upstream_ref[:, cols] * normalized * (1.0 - opened)).astype(BF16))
+    attended.wait()
+    ggate.wait()
 
 
 def query_gradient_kernel(
-    heads, k_ref, v_ref, cum_ref, cumt_ref, grad_ref, prior_ref, gq_ref, mixed_ref
+    heads, q_ref, k_ref, v_ref, cum_ref, cumt_ref, grad_ref, prior_ref, weights_ref,
+    gq_hbm, gk_ref, gv_ref, gq_ref, mixed_ref, sems,
 ):
     length = k_ref.shape[0]
     half = length // 2
     cum = cum_ref[...]
-    for h in range(heads):
-        cols = slice(h * HD, (h + 1) * HD)
-        k, v, grad = k_ref[:, cols], v_ref[:, cols], grad_ref[:, cols]
-        top, bottom = decay_blocks(cum[:, h : h + 1], cumt_ref[h : h + 1])
-        top = (top * dot(grad[:half], v[:half], (1, 1))).astype(BF16)
-        bottom = (bottom * dot(grad[half:], v, (1, 1))).astype(BF16)
-        mixed_ref[h, :half, :half] = top
-        mixed_ref[h, :half, half:] = jnp.zeros((half, length - half), BF16)
-        mixed_ref[h, half:] = bottom
-        gq = jnp.concatenate([dot(top, k[:half]), dot(bottom, k)])
-        gq = gq + jnp.exp(cum[:, h : h + 1]) * dot(grad, prior_ref[h], (1, 1))
-        gq_ref[:, cols] = gq.astype(BF16)
-
-
-def key_part_kernel(heads, q_ref, grad_ref, weights_ref, mixed_ref, gk_ref, gv_ref):
-    for h in range(heads):
-        cols = slice(h * HD, (h + 1) * HD)
-        gk_ref[:, cols] = dot(mixed_ref[h], q_ref[:, cols], (0, 0))
-        gv_ref[:, cols] = dot(weights_ref[h], grad_ref[:, cols], (0, 0))
+    grown = jnp.exp(cum)
+    copies = []
+    for low in (half, 0):
+        rows, seen = slice(low, low + half), slice(0, low + half)
+        for h in range(heads):
+            cols = slice(h * HD, (h + 1) * HD)
+            grad = grad_ref[rows, cols]
+            gap = masked_gap(cum[:, h : h + 1], cumt_ref[h : h + 1], low, low + half, 0, low + half)
+            mixed = (jnp.exp(gap) * dot(grad, v_ref[seen, cols], (1, 1))).astype(BF16)
+            mixed_ref[h, rows, seen] = mixed
+            gq = dot(mixed, k_ref[seen, cols])
+            gq = gq + grown[rows, h : h + 1] * dot(grad, prior_ref[h], (1, 1))
+            gq_ref[rows, cols] = gq.astype(BF16)
+        copy = pltpu.make_async_copy(gq_ref.at[rows], gq_hbm.at[rows], sems.at[len(copies)])
+        copy.start()
+        copies.append(copy)
+    top, bottom = slice(0, half), slice(half, length)
+    for h in range(heads):
+        cols = slice(h * HD, (h + 1) * HD)
+        for held_ref, by_ref, out_ref in ((mixed_ref, q_ref, gk_ref), (weights_ref, grad_ref, gv_ref)):
+            early = dot(held_ref[h, top, top], by_ref[top, cols], (0, 0))
+            late = dot(held_ref[h, bottom], by_ref[bottom, cols], (0, 0))
+            out_ref[top, cols] = early + late[:half]
+            out_ref[bottom, cols] = late[half:]
+    for copy in copies:
+        copy.wait()
 
 
 def key_gradient_kernel(
@@ -326,6 +356,7 @@
     last = cum[length - 1 : length]
     lane = lax.broadcasted_iota(jnp.int32, (length, HD), 1)
     tails = []
+    fades = jnp.exp(last - cum)
     changes = jnp.zeros((length, HD), F32)
     for h in range(heads):
         cols = slice(h * HD, (h + 1) * HD)
@@ -333,7 +364,7 @@
         mine, got = mine_ref[h % half, HD:], got_ref[h % half, HD:]
         own = core == h // half
         ggain_ref[:, cols] = one_of(own, joined_rows(mine), joined_rows(got))
-        fade = jnp.exp(last[:, h : h + 1] - cum[:, h : h + 1])
+        fade = fades[:, h : h + 1]
         pull = fade * dot(v, later, (1, 1))
         gk_part = gk_part_ref[:, cols]
         gk_ref[:, cols] = (gk_part + pull).astype(BF16)
@@ -349,12 +380,17 @@
     gdecayt_ref[...] = tail + sum(dot(part, ones) for part in three_parts(changes.T[:heads]))
 
 
-def local_call(kernel, outs, args, flops=0, moved=0, scratch=()):
+def local_call(kernel, outs, args, flops=0, moved=0, scratch=(), far_out=(), room=40):
+    def spec(far):
+        return pl.BlockSpec(memory_space=pltpu.HBM if far else pltpu.VMEM)
+
     return pl.pallas_call(
         kernel,
         out_shape=[jax.ShapeDtypeStruct(shape, kind) for shape, kind in outs],
+        in_specs=[spec(False)] * len(args),
+        out_specs=[spec(place in far_out) for place in range(len(outs))],
         scratch_shapes=list(scratch),
-        compiler_params=pltpu.CompilerParams(vmem_limit_bytes=40 * 2**20),
+        compiler_params=pltpu.CompilerParams(vmem_limit_bytes=int(room * 2**20)),
         cost_estimate=pl.CostEstimate(flops=flops, bytes_accessed=moved, transcendentals=0),
     )(*args)
 
@@ -380,11 +416,13 @@
     chunks = half * HD // ROWS
     tokens, tokens32 = ((length, width), BF16), ((length, width), F32)
     square = ((heads, length, length), BF16)
+    held = pltpu.VMEM((heads, length, HD), BF16)
     local, theirs, cum, cumt = local_call(
         functools.partial(local_state_kernel, heads),
         [(state, BF16), (carried, BF16), ((length, heads), F32), ((heads, length), F32)],
         (key_rows, value_rows, log_decay.T),
         WORK, WORK // 100,
+        room=53.2,
     )
     got = swap(theirs)
     intra, weights, decayed = local_call(
@@ -393,7 +431,6 @@
         (queries, key_rows, value_rows, cum, cumt),
         WORK, WORK // 100,
     )
-    got, intra = lax.optimization_barrier((got, intra))
     (payload,) = local_call(
         functools.partial(forward_join_kernel, half),
         [((chunks, ROWS + EXTRA, HD), BF16)],
@@ -435,14 +472,10 @@
         [tokens] * 2,
         (opened, upstream, gain, attn, inverse),
         WORK, WORK // 100,
-    )
-    grad_q, mixed = local_call(
-        functools.partial(query_gradient_kernel, heads),
-        [tokens, square],
-        (key_rows, value_rows, cum, cumt, grad, prior),
-        WORK, WORK // 100,
-    )
-    got_back, mixed = lax.optimization_barrier((got_back, mixed))
+        [held, held, pltpu.SemaphoreType.DMA((2 * heads,))],
+        far_out=(0, 1),
+    )
+    got_back, attended = lax.optimization_barrier((got_back, attended))
     (payload,) = local_call(
         functools.partial(backward_join_kernel, half),
         [((chunks, ROWS + EXTRA, HD), BF16)],
@@ -458,11 +491,13 @@
         [(carried, BF16)] * 2,
         (outgoing, got_back, local, cumt, got, scanned, exchange(back)),
     )
-    gk_part, gv_part = local_call(
-        functools.partial(key_part_kernel, heads),
-        [tokens32] * 2,
-        (queries, grad, weights, mixed),
-        WORK, WORK // 100,
+    grad_q, gk_part, gv_part = local_call(
+        functools.partial(query_gradient_kernel, heads),
+        [tokens, tokens32, tokens32],
+        (queries, key_rows, value_rows, cum, cumt, grad, prior, weights),
+        WORK, WORK // 100,
+        [pltpu.VMEM(*tokens), pltpu.VMEM(*square), pltpu.SemaphoreType.DMA((2,))],
+        far_out=(0,),
     )
     grad_k, grad_v, grad_decay, grad_gain = local_call(
         functools.partial(key_gradient_kernel, heads),

time: 96.3 us -> 93.4 us (0.970)
  local copies, waits for them, and re-layouts: 2.8 us -> 0.72 us
    unnamed x18 -> x14, local copies, waits for them, and re-layouts: 2.8 us -> 0.72 us
    pallas_call x15 -> x14, Pallas kernels: 11.8 us -> 12.4 us  [local_call(): pl.pallas_call(kernel, out_shape=[jax.ShapeDtypeStruct(shape, kind) for s...]
where the time goes in v3:
time: 93.4 us; the launch traced here: 93.1 us
  blocking collectives  60.3 us (65%)
  starting transfers between devices  14.6 us (16%)
  Pallas kernels  12.4 us (13%)
  waiting for transfers between devices  4.33 us (5%)
    all_to_all x4, blocking collectives, exchange(): return lax.all_to_all(payload, ('x', 'z'), 0, 0, tiled=True)  60.3 us
    pallas_call x14, Pallas kernels, local_call(): pl.pallas_call(kernel, out_shape=[jax.ShapeDtypeStruct(shape, kind) for s...  12.4 us
    ppermute x4, starting transfers between devices, swap(): return lax.ppermute(value, 'core', [(0, 1), (1, 0)])  11.1 us
    ppermute x3, starting transfers between devices, per_device(): lax.ppermute(sums, 'head', [(i, i ^ step) for i in range(size)])  3.5 us
    ppermute x3, waiting for transfers between devices, per_device(): lax.ppermute(sums, 'head', [(i, i ^ step) for i in range(size)])  3.33 us
  transfers between devices with their start and end apart: 7, of which 3 were waited for; matrix products, arithmetic and copies ran while one was open for 0% of the time, Pallas kernels for 6%

profile of v3, /device:TPU:1, one launch (start us, length us, event | category | flops | bytes accessed | tf_op | source)
XLA Modules:
  0.0 93.1 jit_solution(11734918601476698318)
XLA Ops:
  0.6 0.7 copy-done.6
  1.3 2.4 %shard_map.126 = (bf16[8,128,128]{2,1,0:T(8,128)(2,1)S(1)}, bf16[4,136,128]{2,1,0:T(8,128)(2,1)S(1)}, f32[256,8]{1,0:T(8,128)S(1)}, f32[8,256]{1,0:T(8,128)S(1)}) custom-call(bf16[256,1024]{1,0:T(8,128)(2,1)} %k_ref.7, bf16[256,1024]{1,0:T(8,128)(2,1)} %v_ref.7, f32[8,256]{1,0:T(8,128)S(1)} %bitcast.9), custom_call_target="tpu_custom_call" | custom-call | flops 500000000 | bytes 5000000 | tf_op jit(solution)/shard_map/pallas_call | solution.py:387
  3.7 3.3 %collective-permute-start = (bf16[4,136,128]{2,1,0:T(8,128)(2,1)S(1)}, bf16[4,136,128]{2,1,0:T(8,128)(2,1)S(1)}, u32[]{:S(2)}, u32[]{:S(2)}) collective-permute-start(bf16[4,136,128]{2,1,0:T(8,128)(2,1)S(1)} %get-tuple-element.49), channel_id=1, source_target_pairs={{0,4},{4,0},{1,5},{5,1},{2,6},{6,2},{3,7},{7,3},{8,12},{12,8},{9,1... | collective-permute-start | bytes 417800 | tf_op jit(solution)/shard_map/ppermute | solution.py:403
  7.1 1.0 %collective-permute-done.got_ref.got_state_ref = bf16[4,136,128]{2,1,0:T(8,128)(2,1)S(1)} collective-permute-done((bf16[4,136,128]{2,1,0:T(8,128)(2,1)S(1)}, bf16[4,136,128]{2,1,0:T(8,128)(2,1)S(1)}, u32[]{:S(2)}, u32[]{:S(2)}) %collective-permute-start) | collective-permute-done | bytes 139296 | tf_op jit(solution)/shard_map/ppermute | solution.py:403
  8.1 0.1 shard_map.129
  8.2 0.0 copy-start.1
  8.2 18.6 %all_to_all.20.pay_ref = bf16[32,24,128]{2,1,0:T(8,128)(2,1)S(1)} all-to-all(bf16[32,24,128]{2,1,0:T(8,128)(2,1)S(1)} %shard_map.129), channel_id=1, replica_groups=mesh['x'=4,'z'=8,'core'=2,'head'=4] {'x','z'}, dimensions={0} | all-to-all | bytes 393216 | tf_op jit(solution)/shard_map/all_to_all | solution.py:399
  26.8 0.1 shard_map.130
  26.9 14.5 %all_to_all.21 = bf16[32,16,128]{2,1,0:T(8,128)(2,1)S(1)} all-to-all(bf16[32,16,128]{2,1,0:T(8,128)(2,1)S(1)} %get-tuple-element.50), channel_id=1, replica_groups=mesh['x'=4,'z'=8,'core'=2,'head'=4] {'x','z'}, dimensions={0} | all-to-all | bytes 262144 | tf_op jit(solution)/shard_map/all_to_all | solution.py:399
  41.4 0.1 shard_map.131
  41.6 2.9 %collective-permute-start.1 = (bf16[4,128,128]{2,1,0:T(8,128)(2,1)S(1)}, bf16[4,128,128]{2,1,0:T(8,128)(2,1)S(1)}, u32[]{:S(2)}, u32[]{:S(2)}) collective-permute-start(bf16[4,128,128]{2,1,0:T(8,128)(2,1)S(1)} %get-tuple-element.52), channel_id=1, source_target_pairs={{0,4},{4,0},{1,5},{5,1},{2,6},{6,2},{3,7},{7,3},{8,12},{12,8},{9,1... | collective-permute-start | bytes 393224 | tf_op jit(solution)/shard_map/ppermute | solution.py:403
  44.5 0.0 copy-start.4
  44.5 0.0 copy-start.5
  44.6 1.4 %shard_map.127 = (f32[256,1024]{1,0:T(8,128)S(1)}, bf16[8,256,256]{2,1,0:T(8,128)(2,1)S(1)}, bf16[256,1024]{1,0:T(8,128)(2,1)S(1)}) custom-call(bf16[256,1024]{1,0:T(8,128)(2,1)S(1)} %copy-done.2, bf16[256,1024]{1,0:T(8,128)(2,1)S(1)} %copy-done, bf16[256,1024]{1,0:T(8,128)(2,1)S(1)} %copy-done.1, f32[256,8]{1,0:T(8,128)S(1)} %get-tuple-element.42.cum_ref, ...), custom_call_target="tpu_custom_call" | custom-call | flops 500000000 | bytes 5000000 | tf_op jit(solution)/shard_map/pallas_call | solution.py:387
  46.0 0.2 shard_map.128
  46.3 0.5 shard_map.132
  46.8 2.8 %collective-permute-start.4 = (f32[8,256]{1,0:T(8,128)S(1)}, f32[8,256]{1,0:T(8,128)S(1)}, u32[]{:S(2)}, u32[]{:S(2)}) collective-permute-start(f32[8,256]{1,0:T(8,128)S(1)} %get-tuple-element.54.sums0_ref), channel_id=1, source_target_pairs={{0,3},{1,2},{2,1},{3,0},{4,7},{5,6},{6,5},{7,4},{8,11},{9,10},{10,... | collective-permute-start | bytes 24584 | tf_op jit(solution)/shard_map/ppermute | solution.py:460
  49.6 0.3 collective-permute-start.3
  50.0 0.3 collective-permute-start.2
  50.3 0.4 collective-permute-done.4.sums3_ref
  50.6 3.0 %collective-permute-done.3.sums2_ref = f32[8,256]{1,0:T(8,128)S(1)} collective-permute-done((f32[8,256]{1,0:T(8,128)S(1)}, f32[8,256]{1,0:T(8,128)S(1)}, u32[]{:S(2)}, u32[]{:S(2)}) %collective-permute-start.3) | collective-permute-done | bytes 8224 | tf_op jit(solution)/shard_map/ppermute | solution.py:460
  53.6 0.8 shard_map.133
  54.4 1.6 %collective-permute-start.5 = (f32[4,136,128]{2,1,0:T(8,128)S(1)}, f32[4,136,128]{2,1,0:T(8,128)S(1)}, u32[]{:S(2)}, u32[]{:S(2)}) collective-permute-start(f32[4,136,128]{2,1,0:T(8,128)S(1)} %get-tuple-element.55), channel_id=1, source_target_pairs={{0,4},{4,0},{1,5},{5,1},{2,6},{6,2},{3,7},{7,3},{8,12},{12,8},{9,1... | collective-permute-start | bytes 835592 | tf_op jit(solution)/shard_map/ppermute | solution.py:403
  56.0 1.2 %shard_map.134 = (bf16[256,1024]{1,0:T(8,128)(2,1)}, bf16[256,1024]{1,0:T(8,128)(2,1)}) custom-call(f32[256,1024]{1,0:T(8,128)S(1)} %get-tuple-element.45.opened_ref, f32[256,1024]{1,0:T(8,128)S(1)} %get-tuple-element.46.upstream_ref, f32[1,1024]{1,0:T(1,128)S(1)} %bitcast.8, f32[256,1024]{1,0:T(8,128)S(1)} %get-tuple-element.53.attn_ref, ...), custom_call_target="tpu_custom_call" | custom-call | flops 500000000 | bytes 5000000 | tf_op jit(solution)/shard_map/pallas_call | solution.py:387
  57.2 0.1 shard_map.136
  57.4 12.5 %all_to_all.22.pay_ref = bf16[32,24,128]{2,1,0:T(8,128)(2,1)S(1)} all-to-all(bf16[32,24,128]{2,1,0:T(8,128)(2,1)S(1)} %shard_map.136), channel_id=1, replica_groups=mesh['x'=4,'z'=8,'core'=2,'head'=4] {'x','z'}, dimensions={0} | all-to-all | bytes 393216 | tf_op jit(solution)/shard_map/all_to_all | solution.py:399
  69.9 0.2 shard_map.137
  70.0 14.7 %all_to_all.23.back_ref = bf16[32,24,128]{2,1,0:T(8,128)(2,1)S(1)} all-to-all(bf16[32,24,128]{2,1,0:T(8,128)(2,1)S(1)} %shard_map.137), channel_id=1, replica_groups=mesh['x'=4,'z'=8,'core'=2,'head'=4] {'x','z'}, dimensions={0} | all-to-all | bytes 393216 | tf_op jit(solution)/shard_map/all_to_all | solution.py:399
  84.7 0.2 shard_map.138
  84.9 3.3 %collective-permute-start.6 = (bf16[4,136,128]{2,1,0:T(8,128)(2,1)S(1)}, bf16[4,136,128]{2,1,0:T(8,128)(2,1)S(1)}, u32[]{:S(2)}, u32[]{:S(2)}) collective-permute-start(bf16[4,136,128]{2,1,0:T(8,128)(2,1)S(1)} %get-tuple-element.71), channel_id=1, source_target_pairs={{0,4},{4,0},{1,5},{5,1},{2,6},{6,2},{3,7},{7,3},{8,12},{12,8},{9,1... | collective-permute-start | bytes 417800 | tf_op jit(solution)/shard_map/ppermute | solution.py:403
  88.2 2.6 %shard_map.135 = (bf16[256,1024]{1,0:T(8,128)(2,1)}, f32[256,1024]{1,0:T(8,128)S(1)}, f32[256,1024]{1,0:T(8,128)S(1)}) custom-call(bf16[256,1024]{1,0:T(8,128)(2,1)S(1)} %copy-done.2, bf16[256,1024]{1,0:T(8,128)(2,1)S(1)} %copy-done, bf16[256,1024]{1,0:T(8,128)(2,1)S(1)} %copy-done.1, f32[256,8]{1,0:T(8,128)S(1)} %get-tuple-element.42.cum_ref, ...), custom_call_target="tpu_custom_call" | custom-call | flops 500000000 | bytes 5000000 | tf_op jit(solution)/shard_map/pallas_call | solution.py:387
  90.8 2.3 %shard_map.139 = (bf16[256,1024]{1,0:T(8,128)(2,1)}, bf16[256,1024]{1,0:T(8,128)(2,1)}, f32[8,256]{1,0:T(8,128)}, f32[1,1024]{1,0:T(1,128)}) custom-call(bf16[256,1024]{1,0:T(8,128)(2,1)S(1)} %copy-done, bf16[256,1024]{1,0:T(8,128)(2,1)S(1)} %copy-done.1, f32[256,8]{1,0:T(8,128)S(1)} %get-tuple-element.42.cum_ref, ...), custom_call_target="tpu_custom_call" | custom-call | flops 500000000 | bytes 5000000 | tf_op jit(solution)/shard_map/pallas_call | solution.py:387
  (14 shorter events, 0.0 us)
Async XLA Ops:
  0.6 0.7 copy-start.6
  3.7 4.3 %collective-permute-start = (bf16[4,136,128]{2,1,0:T(8,128)(2,1)S(1)}, bf16[4,136,128]{2,1,0:T(8,128)(2,1)S(1)}, u32[]{:S(2)}, u32[]{:S(2)}) collective-permute-start(bf16[4,136,128]{2,1,0:T(8,128)(2,1)S(1)} %get-tuple-element.49), channel_id=1, source_target_pairs={{0,4},{4,0},{1,5},{5,1},{2,6},{6,2},{3,7},{7,3},{8,12},{12,8},{9,1... | collective-permute-start | bytes 417800 | tf_op jit(solution)/shard_map/ppermute | solution.py:403
  8.1 36.5 %copy-start.2 = (bf16[256,1024]{1,0:T(8,128)(2,1)S(1)}, bf16[256,1024]{1,0:T(8,128)(2,1)}, u32[]{:S(2)}) copy-start(bf16[256,1024]{1,0:T(8,128)(2,1)} %q_ref.3) | copy-start | bytes 1572868
  8.2 36.3 %copy-start.1 = (bf16[256,1024]{1,0:T(8,128)(2,1)S(1)}, bf16[256,1024]{1,0:T(8,128)(2,1)}, u32[]{:S(2)}) copy-start(bf16[256,1024]{1,0:T(8,128)(2,1)} %v_ref.7) | copy-start | bytes 1572868
  26.8 17.7 %copy-start = (bf16[256,1024]{1,0:T(8,128)(2,1)S(1)}, bf16[256,1024]{1,0:T(8,128)(2,1)}, u32[]{:S(2)}) copy-start(bf16[256,1024]{1,0:T(8,128)(2,1)} %k_ref.7) | copy-start | bytes 1572868
  41.6 4.7 %collective-permute-start.1 = (bf16[4,128,128]{2,1,0:T(8,128)(2,1)S(1)}, bf16[4,128,128]{2,1,0:T(8,128)(2,1)S(1)}, u32[]{:S(2)}, u32[]{:S(2)}) collective-permute-start(bf16[4,128,128]{2,1,0:T(8,128)(2,1)S(1)} %get-tuple-element.52), channel_id=1, source_target_pairs={{0,4},{4,0},{1,5},{5,1},{2,6},{6,2},{3,7},{7,3},{8,12},{12,8},{9,1... | collective-permute-start | bytes 393224 | tf_op jit(solution)/shard_map/ppermute | solution.py:403
  44.5 1.5 %copy-start.3 = (bf16[256,1024]{1,0:T(8,128)(2,1)S(1)}, bf16[256,1024]{1,0:T(8,128)(2,1)}, u32[]{:S(2)}) copy-start(bf16[256,1024]{1,0:T(8,128)(2,1)} %cot_ref.3) | copy-start | bytes 1572868
  44.5 1.5 %copy-start.4 = (f32[1024]{0:T(1024)S(1)}, f32[1024]{0:T(1024)}, u32[]{:S(2)}) copy-start(f32[1024]{0:T(1024)} %param.11) | copy-start | bytes 12292
  44.5 1.5 %copy-start.5 = (bf16[256,1024]{1,0:T(8,128)(2,1)S(1)}, bf16[256,1024]{1,0:T(8,128)(2,1)}, u32[]{:S(2)}) copy-start(bf16[256,1024]{1,0:T(8,128)(2,1)} %gate_ref.1) | copy-start | bytes 1572868
  46.8 3.9 %collective-permute-start.4 = (f32[8,256]{1,0:T(8,128)S(1)}, f32[8,256]{1,0:T(8,128)S(1)}, u32[]{:S(2)}, u32[]{:S(2)}) collective-permute-start(f32[8,256]{1,0:T(8,128)S(1)} %get-tuple-element.54.sums0_ref), channel_id=1, source_target_pairs={{0,3},{1,2},{2,1},{3,0},{4,7},{5,6},{6,5},{7,4},{8,11},{9,10},{10,... | collective-permute-start | bytes 24584 | tf_op jit(solution)/shard_map/ppermute | solution.py:460
  49.6 4.0 %collective-permute-start.3 = (f32[8,256]{1,0:T(8,128)S(1)}, f32[8,256]{1,0:T(8,128)S(1)}, u32[]{:S(2)}, u32[]{:S(2)}) collective-permute-start(f32[8,256]{1,0:T(8,128)S(1)} %get-tuple-element.54.sums0_ref), channel_id=1, source_target_pairs={{0,2},{1,3},{2,0},{3,1},{4,6},{5,7},{6,4},{7,5},{8,10},{9,11},{10,... | collective-permute-start | bytes 24584 | tf_op jit(solution)/shard_map/ppermute | solution.py:460
  50.0 3.7 %collective-permute-start.2 = (f32[8,256]{1,0:T(8,128)S(1)}, f32[8,256]{1,0:T(8,128)S(1)}, u32[]{:S(2)}, u32[]{:S(2)}) collective-permute-start(f32[8,256]{1,0:T(8,128)S(1)} %get-tuple-element.54.sums0_ref), channel_id=1, source_target_pairs={{0,1},{1,0},{2,3},{3,2},{4,5},{5,4},{6,7},{7,6},{8,9},{9,8},{10,11... | collective-permute-start | bytes 24584 | tf_op jit(solution)/shard_map/ppermute | solution.py:460
  54.4 2.8 %collective-permute-start.5 = (f32[4,136,128]{2,1,0:T(8,128)S(1)}, f32[4,136,128]{2,1,0:T(8,128)S(1)}, u32[]{:S(2)}, u32[]{:S(2)}) collective-permute-start(f32[4,136,128]{2,1,0:T(8,128)S(1)} %get-tuple-element.55), channel_id=1, source_target_pairs={{0,4},{4,0},{1,5},{5,1},{2,6},{6,2},{3,7},{7,3},{8,12},{12,8},{9,1... | collective-permute-start | bytes 835592 | tf_op jit(solution)/shard_map/ppermute | solution.py:403
  84.9 5.9 %collective-permute-start.6 = (bf16[4,136,128]{2,1,0:T(8,128)(2,1)S(1)}, bf16[4,136,128]{2,1,0:T(8,128)(2,1)S(1)}, u32[]{:S(2)}, u32[]{:S(2)}) collective-permute-start(bf16[4,136,128]{2,1,0:T(8,128)(2,1)S(1)} %get-tuple-element.71), channel_id=1, source_target_pairs={{0,4},{4,0},{1,5},{5,1},{2,6},{6,2},{3,7},{7,3},{8,12},{12,8},{9,1... | collective-permute-start | bytes 417800 | tf_op jit(solution)/shard_map/ppermute | solution.py:403

commit v4 on v3

--- a/solution.py
+++ b/solution.py
@@ -77,10 +77,24 @@
     return jnp.where(first, if_first, if_second)
 
 
-def local_state_kernel(heads, k_ref, v_ref, ldt_ref, loc_ref, theirs_ref, cum_ref, cumt_ref):
+def local_state_kernel(
+    heads, k_hbm, v_hbm, ldt_hbm, loc_ref, theirs_ref, cum_ref, cumt_ref,
+    k_ref, v_ref, ldt_ref, sum_ref, sems,
+):
     length = k_ref.shape[0]
     half = heads // 2
-    core = lax.axis_index("core")
+    split = length // 2
+    core = lax.axis_index("core")
+    logs = pltpu.make_async_copy(ldt_hbm, ldt_ref, sems.at[4])
+    logs.start()
+    copies = []
+    for part in range(2):
+        rows = slice(part * split, (part + 1) * split)
+        for far, near in ((k_hbm, k_ref), (v_hbm, v_ref)):
+            copies.append(pltpu.make_async_copy(far.at[rows], near.at[rows], sems.at[len(copies)]))
+    for copy in copies:
+        copy.start()
+    logs.wait()
     ones = triangle_bf(length, True)
     cumt = sum(dot(part, ones) for part in three_parts(ldt_ref[...]))
     cumt_ref[...] = cumt
@@ -88,10 +102,18 @@
     cum_ref[...] = cum
     last = cum[length - 1 : length]
     fade = jnp.exp(last - cum)
-    for h in range(heads):
-        cols = slice(h * HD, (h + 1) * HD)
-        decayed = (k_ref[:, cols].astype(F32) * fade[:, h : h + 1]).astype(BF16)
-        loc_ref[h] = dot(decayed, v_ref[:, cols], (0, 0)).astype(BF16)
+    for part in range(2):
+        rows = slice(part * split, (part + 1) * split)
+        copies[2 * part].wait()
+        copies[2 * part + 1].wait()
+        for h in range(heads):
+            cols = slice(h * HD, (h + 1) * HD)
+            decayed = (k_ref[rows, cols].astype(F32) * fade[rows, h : h + 1]).astype(BF16)
+            value = dot(decayed, v_ref[rows, cols], (0, 0))
+            if part == 0:
+                sum_ref[h] = value
+            else:
+                loc_ref[h] = (sum_ref[h] + value).astype(BF16)
     theirs_ref[:, :HD] = loc_ref[pl.ds((1 - core) * half, half)]
     for h in range(half):
         value = one_of(core == 0, last[:, half + h : half + h + 1], last[:, h : h + 1])
@@ -215,23 +237,26 @@
         theirs_ref[h, HD:] = small_rows(gain, one_of(core == 0, meet1, meet0))
 
 
+def masked_bf(masks, scores):
+    top, bottom = masks
+    half = top.shape[0]
+    upper = (top * scores[:half, :half]).astype(BF16)
+    lower = (bottom * scores[half:]).astype(BF16)
+    empty = jnp.zeros((half, scores.shape[1] - half), BF16)
+    return jnp.concatenate([jnp.concatenate([upper, empty], axis=1), lower])
+
+
 def within_kernel(heads, q_ref, k_ref, v_ref, cum_ref, cumt_ref, intra_ref, weights_ref, decayed_ref):
-    length = q_ref.shape[0]
-    half = length // 2
     cum = cum_ref[...]
     grown = jnp.exp(cum)
     for h in range(heads):
         cols = slice(h * HD, (h + 1) * HD)
-        q, k, v = q_ref[:, cols], k_ref[:, cols], v_ref[:, cols]
-        top, bottom = decay_blocks(cum[:, h : h + 1], cumt_ref[h : h + 1])
-        top = (top * dot(q[:half], k[:half], (1, 1))).astype(BF16)
-        bottom = (bottom * dot(q[half:], k, (1, 1))).astype(BF16)
-        weights_ref[h, :half, :half] = top
-        weights_ref[h, :half, half:] = jnp.zeros((half, length - half), BF16)
-        weights_ref[h, half:] = bottom
+        q = q_ref[:, cols]
+        masks = decay_blocks(cum[:, h : h + 1], cumt_ref[h : h + 1])
+        weights = masked_bf(masks, dot(q, k_ref[:, cols], (1, 1)))
+        weights_ref[h] = weights
         decayed_ref[:, cols] = (q.astype(F32) * grown[:, h : h + 1]).astype(BF16)
-        intra_ref[:half, cols] = dot(top, v[:half])
-        intra_ref[half:, cols] = dot(bottom, v)
+        intra_ref[:, cols] = dot(weights, v_ref[:, cols])
 
 
 def gate_kernel(gate_ref, cot_ref, gain_ref, opened_ref, upstream_ref):
@@ -310,37 +335,26 @@
 
 def query_gradient_kernel(
     heads, q_ref, k_ref, v_ref, cum_ref, cumt_ref, grad_ref, prior_ref, weights_ref,
-    gq_hbm, gk_ref, gv_ref, gq_ref, mixed_ref, sems,
-):
-    length = k_ref.shape[0]
-    half = length // 2
+    gq_hbm, gk_ref, gv_ref, gq_ref, mixed_ref, sem,
+):
     cum = cum_ref[...]
     grown = jnp.exp(cum)
-    copies = []
-    for low in (half, 0):
-        rows, seen = slice(low, low + half), slice(0, low + half)
-        for h in range(heads):
-            cols = slice(h * HD, (h + 1) * HD)
-            grad = grad_ref[rows, cols]
-            gap = masked_gap(cum[:, h : h + 1], cumt_ref[h : h + 1], low, low + half, 0, low + half)
-            mixed = (jnp.exp(gap) * dot(grad, v_ref[seen, cols], (1, 1))).astype(BF16)
-            mixed_ref[h, rows, seen] = mixed
-            gq = dot(mixed, k_ref[seen, cols])
-            gq = gq + grown[rows, h : h + 1] * dot(grad, prior_ref[h], (1, 1))
-            gq_ref[rows, cols] = gq.astype(BF16)
-        copy = pltpu.make_async_copy(gq_ref.at[rows], gq_hbm.at[rows], sems.at[len(copies)])
-        copy.start()
-        copies.append(copy)
-    top, bottom = slice(0, half), slice(half, length)
-    for h in range(heads):
-        cols = slice(h * HD, (h + 1) * HD)
-        for held_ref, by_ref, out_ref in ((mixed_ref, q_ref, gk_ref), (weights_ref, grad_ref, gv_ref)):
-            early = dot(held_ref[h, top, top], by_ref[top, cols], (0, 0))
-            late = dot(held_ref[h, bottom], by_ref[bottom, cols], (0, 0))
-            out_ref[top, cols] = early + late[:half]
-            out_ref[bottom, cols] = late[half:]
-    for copy in copies:
-        copy.wait()
+    for h in range(heads):
+        cols = slice(h * HD, (h + 1) * HD)
+        grad = grad_ref[:, cols]
+        masks = decay_blocks(cum[:, h : h + 1], cumt_ref[h : h + 1])
+        mixed = masked_bf(masks, dot(grad, v_ref[:, cols], (1, 1)))
+        mixed_ref[h] = mixed
+        gq = dot(mixed, k_ref[:, cols])
+        gq = gq + grown[:, h : h + 1] * dot(grad, prior_ref[h], (1, 1))
+        gq_ref[:, cols] = gq.astype(BF16)
+    copy = pltpu.make_async_copy(gq_ref, gq_hbm, sem)
+    copy.start()
+    for h in range(heads):
+        cols = slice(h * HD, (h + 1) * HD)
+        gk_ref[:, cols] = dot(mixed_ref[h], q_ref[:, cols], (0, 0))
+        gv_ref[:, cols] = dot(weights_ref[h], grad_ref[:, cols], (0, 0))
+    copy.wait()
 
 
 def key_gradient_kernel(
@@ -380,14 +394,14 @@
     gdecayt_ref[...] = tail + sum(dot(part, ones) for part in three_parts(changes.T[:heads]))
 
 
-def local_call(kernel, outs, args, flops=0, moved=0, scratch=(), far_out=(), room=40):
+def local_call(kernel, outs, args, flops=0, moved=0, scratch=(), far_in=(), far_out=(), room=40):
     def spec(far):
         return pl.BlockSpec(memory_space=pltpu.HBM if far else pltpu.VMEM)
 
     return pl.pallas_call(
         kernel,
         out_shape=[jax.ShapeDtypeStruct(shape, kind) for shape, kind in outs],
-        in_specs=[spec(False)] * len(args),
+        in_specs=[spec(place in far_in) for place in range(len(args))],
         out_specs=[spec(place in far_out) for place in range(len(outs))],
         scratch_shapes=list(scratch),
         compiler_params=pltpu.CompilerParams(vmem_limit_bytes=int(room * 2**20)),
@@ -422,6 +436,11 @@
         [(state, BF16), (carried, BF16), ((length, heads), F32), ((heads, length), F32)],
         (key_rows, value_rows, log_decay.T),
         WORK, WORK // 100,
+        [
+            pltpu.VMEM(*tokens), pltpu.VMEM(*tokens), pltpu.VMEM((heads, length), F32),
+            pltpu.VMEM(state, F32), pltpu.SemaphoreType.DMA((5,)),
+        ],
+        far_in=(0, 1, 2),
         room=53.2,
     )
     got = swap(theirs)
@@ -496,7 +515,7 @@
         [tokens, tokens32, tokens32],
         (queries, key_rows, value_rows, cum, cumt, grad, prior, weights),
         WORK, WORK // 100,
-        [pltpu.VMEM(*tokens), pltpu.VMEM(*square), pltpu.SemaphoreType.DMA((2,))],
+        [pltpu.VMEM(*tokens), pltpu.VMEM(*square), pltpu.SemaphoreType.DMA],
         far_out=(0,),
     )
     grad_k, grad_v, grad_decay, grad_gain = local_call(

time: 93.4 us -> 92.5 us (level)
  Pallas kernels: 12.4 us -> 11.2 us
    pallas_call x14, Pallas kernels: 12.4 us -> 11.2 us  [local_call(): pl.pallas_call(kernel, out_shape=[jax.ShapeDtypeStruct(shape, kind) for s...]
  transfers between devices with their start and end apart: 7 -> 7, of which waited for: 3 -> 3; matrix products, arithmetic and copies ran while one was open for 0% -> 0% of each run, Pallas kernels for 6% -> 5%
where the time goes in v4:
time: 92.5 us; the launch traced here: 92.1 us
  blocking collectives  60.3 us (65%)
  starting transfers between devices  14.6 us (16%)
  Pallas kernels  11.2 us (12%)
  waiting for transfers between devices  4.33 us (5%)
    all_to_all x4, blocking collectives, exchange(): return lax.all_to_all(payload, ('x', 'z'), 0, 0, tiled=True)  60.3 us
    pallas_call x14, Pallas kernels, local_call(): pl.pallas_call(kernel, out_shape=[jax.ShapeDtypeStruct(shape, kind) for s...  11.2 us
    ppermute x4, starting transfers between devices, swap(): return lax.ppermute(value, 'core', [(0, 1), (1, 0)])  11.1 us
    ppermute x3, starting transfers between devices, per_device(): lax.ppermute(sums, 'head', [(i, i ^ step) for i in range(size)])  3.5 us
    ppermute x3, waiting for transfers between devices, per_device(): lax.ppermute(sums, 'head', [(i, i ^ step) for i in range(size)])  3.33 us
  transfers between devices with their start and end apart: 7, of which 3 were waited for; matrix products, arithmetic and copies ran while one was open for 0% of the time, Pallas kernels for 5%

profile of v4, /device:TPU:1, one launch (start us, length us, event | category | flops | bytes accessed | tf_op | source)
XLA Modules:
  0.0 92.1 jit_solution(14710509705147824625)
XLA Ops:
  0.6 0.7 copy-done.6
  1.3 2.1 %shard_map.126 = (bf16[8,128,128]{2,1,0:T(8,128)(2,1)S(1)}, bf16[4,136,128]{2,1,0:T(8,128)(2,1)S(1)}, f32[256,8]{1,0:T(8,128)S(1)}, f32[8,256]{1,0:T(8,128)S(1)}) custom-call(bf16[256,1024]{1,0:T(8,128)(2,1)} %k_ref.5, bf16[256,1024]{1,0:T(8,128)(2,1)} %v_ref.5, f32[8,256]{1,0:T(8,128)S(1)} %bitcast.9), custom_call_target="tpu_custom_call" | custom-call | flops 500000000 | bytes 5000000 | tf_op jit(solution)/shard_map/pallas_call | solution.py:401
  3.5 3.4 %collective-permute-start = (bf16[4,136,128]{2,1,0:T(8,128)(2,1)S(1)}, bf16[4,136,128]{2,1,0:T(8,128)(2,1)S(1)}, u32[]{:S(2)}, u32[]{:S(2)}) collective-permute-start(bf16[4,136,128]{2,1,0:T(8,128)(2,1)S(1)} %get-tuple-element.49), channel_id=1, source_target_pairs={{0,4},{4,0},{1,5},{5,1},{2,6},{6,2},{3,7},{7,3},{8,12},{12,8},{9,1... | collective-permute-start | bytes 417800 | tf_op jit(solution)/shard_map/ppermute | solution.py:417
  6.8 1.0 %collective-permute-done.got_ref.got_state_ref = bf16[4,136,128]{2,1,0:T(8,128)(2,1)S(1)} collective-permute-done((bf16[4,136,128]{2,1,0:T(8,128)(2,1)S(1)}, bf16[4,136,128]{2,1,0:T(8,128)(2,1)S(1)}, u32[]{:S(2)}, u32[]{:S(2)}) %collective-permute-start) | collective-permute-done | bytes 139296 | tf_op jit(solution)/shard_map/ppermute | solution.py:417
  7.8 0.1 shard_map.129
  7.9 0.0 copy-start.1
  8.0 18.6 %all_to_all.20.pay_ref = bf16[32,24,128]{2,1,0:T(8,128)(2,1)S(1)} all-to-all(bf16[32,24,128]{2,1,0:T(8,128)(2,1)S(1)} %shard_map.129), channel_id=1, replica_groups=mesh['x'=4,'z'=8,'core'=2,'head'=4] {'x','z'}, dimensions={0} | all-to-all | bytes 393216 | tf_op jit(solution)/shard_map/all_to_all | solution.py:413
  26.6 0.1 shard_map.130
  26.7 14.5 %all_to_all.21 = bf16[32,16,128]{2,1,0:T(8,128)(2,1)S(1)} all-to-all(bf16[32,16,128]{2,1,0:T(8,128)(2,1)S(1)} %get-tuple-element.50), channel_id=1, replica_groups=mesh['x'=4,'z'=8,'core'=2,'head'=4] {'x','z'}, dimensions={0} | all-to-all | bytes 262144 | tf_op jit(solution)/shard_map/all_to_all | solution.py:413
  41.2 0.1 shard_map.131
  41.3 2.9 %collective-permute-start.1 = (bf16[4,128,128]{2,1,0:T(8,128)(2,1)S(1)}, bf16[4,128,128]{2,1,0:T(8,128)(2,1)S(1)}, u32[]{:S(2)}, u32[]{:S(2)}) collective-permute-start(bf16[4,128,128]{2,1,0:T(8,128)(2,1)S(1)} %get-tuple-element.52), channel_id=1, source_target_pairs={{0,4},{4,0},{1,5},{5,1},{2,6},{6,2},{3,7},{7,3},{8,12},{12,8},{9,1... | collective-permute-start | bytes 393224 | tf_op jit(solution)/shard_map/ppermute | solution.py:417
  44.3 1.0 %shard_map.127 = (f32[256,1024]{1,0:T(8,128)S(1)}, bf16[8,256,256]{2,1,0:T(8,128)(2,1)S(1)}, bf16[256,1024]{1,0:T(8,128)(2,1)S(1)}) custom-call(bf16[256,1024]{1,0:T(8,128)(2,1)S(1)} %copy-done.2, bf16[256,1024]{1,0:T(8,128)(2,1)S(1)} %copy-done, bf16[256,1024]{1,0:T(8,128)(2,1)S(1)} %copy-done.1, f32[256,8]{1,0:T(8,128)S(1)} %get-tuple-element.42.cum_ref, ...), custom_call_target="tpu_custom_call" | custom-call | flops 500000000 | bytes 5000000 | tf_op jit(solution)/shard_map/pallas_call | solution.py:401
  45.3 0.0 copy-done.3
  45.3 0.2 copy-done.5
  45.5 0.2 shard_map.128
  45.8 0.5 shard_map.132
  46.3 2.8 %collective-permute-start.4 = (f32[8,256]{1,0:T(8,128)S(1)}, f32[8,256]{1,0:T(8,128)S(1)}, u32[]{:S(2)}, u32[]{:S(2)}) collective-permute-start(f32[8,256]{1,0:T(8,128)S(1)} %get-tuple-element.54.sums0_ref), channel_id=1, source_target_pairs={{0,3},{1,2},{2,1},{3,0},{4,7},{5,6},{6,5},{7,4},{8,11},{9,10},{10,... | collective-permute-start | bytes 24584 | tf_op jit(solution)/shard_map/ppermute | solution.py:479
  49.1 0.3 collective-permute-start.3
  49.4 0.3 collective-permute-start.2
  49.8 0.4 collective-permute-done.4.sums3_ref
  50.1 3.0 %collective-permute-done.3.sums2_ref = f32[8,256]{1,0:T(8,128)S(1)} collective-permute-done((f32[8,256]{1,0:T(8,128)S(1)}, f32[8,256]{1,0:T(8,128)S(1)}, u32[]{:S(2)}, u32[]{:S(2)}) %collective-permute-start.3) | collective-permute-done | bytes 8224 | tf_op jit(solution)/shard_map/ppermute | solution.py:479
  53.1 0.8 shard_map.133
  53.9 1.6 %collective-permute-start.5 = (f32[4,136,128]{2,1,0:T(8,128)S(1)}, f32[4,136,128]{2,1,0:T(8,128)S(1)}, u32[]{:S(2)}, u32[]{:S(2)}) collective-permute-start(f32[4,136,128]{2,1,0:T(8,128)S(1)} %get-tuple-element.55), channel_id=1, source_target_pairs={{0,4},{4,0},{1,5},{5,1},{2,6},{6,2},{3,7},{7,3},{8,12},{12,8},{9,1... | collective-permute-start | bytes 835592 | tf_op jit(solution)/shard_map/ppermute | solution.py:417
  55.5 1.2 %shard_map.134 = (bf16[256,1024]{1,0:T(8,128)(2,1)}, bf16[256,1024]{1,0:T(8,128)(2,1)}) custom-call(f32[256,1024]{1,0:T(8,128)S(1)} %get-tuple-element.45.opened_ref, f32[256,1024]{1,0:T(8,128)S(1)} %get-tuple-element.46.upstream_ref, f32[1,1024]{1,0:T(1,128)S(1)} %bitcast.8, f32[256,1024]{1,0:T(8,128)S(1)} %get-tuple-element.53.attn_ref, ...), custom_call_target="tpu_custom_call" | custom-call | flops 500000000 | bytes 5000000 | tf_op jit(solution)/shard_map/pallas_call | solution.py:401
  56.7 0.1 shard_map.136
  56.9 12.5 %all_to_all.22.pay_ref = bf16[32,24,128]{2,1,0:T(8,128)(2,1)S(1)} all-to-all(bf16[32,24,128]{2,1,0:T(8,128)(2,1)S(1)} %shard_map.136), channel_id=1, replica_groups=mesh['x'=4,'z'=8,'core'=2,'head'=4] {'x','z'}, dimensions={0} | all-to-all | bytes 393216 | tf_op jit(solution)/shard_map/all_to_all | solution.py:413
  69.4 0.2 shard_map.137
  69.5 14.7 %all_to_all.23.back_ref = bf16[32,24,128]{2,1,0:T(8,128)(2,1)S(1)} all-to-all(bf16[32,24,128]{2,1,0:T(8,128)(2,1)S(1)} %shard_map.137), channel_id=1, replica_groups=mesh['x'=4,'z'=8,'core'=2,'head'=4] {'x','z'}, dimensions={0} | all-to-all | bytes 393216 | tf_op jit(solution)/shard_map/all_to_all | solution.py:413
  84.2 0.2 shard_map.138
  84.4 3.3 %collective-permute-start.6 = (bf16[4,136,128]{2,1,0:T(8,128)(2,1)S(1)}, bf16[4,136,128]{2,1,0:T(8,128)(2,1)S(1)}, u32[]{:S(2)}, u32[]{:S(2)}) collective-permute-start(bf16[4,136,128]{2,1,0:T(8,128)(2,1)S(1)} %get-tuple-element.71), channel_id=1, source_target_pairs={{0,4},{4,0},{1,5},{5,1},{2,6},{6,2},{3,7},{7,3},{8,12},{12,8},{9,1... | collective-permute-start | bytes 417800 | tf_op jit(solution)/shard_map/ppermute | solution.py:417
  87.7 2.2 %shard_map.135 = (bf16[256,1024]{1,0:T(8,128)(2,1)}, f32[256,1024]{1,0:T(8,128)S(1)}, f32[256,1024]{1,0:T(8,128)S(1)}) custom-call(bf16[256,1024]{1,0:T(8,128)(2,1)S(1)} %copy-done.2, bf16[256,1024]{1,0:T(8,128)(2,1)S(1)} %copy-done, bf16[256,1024]{1,0:T(8,128)(2,1)S(1)} %copy-done.1, f32[256,8]{1,0:T(8,128)S(1)} %get-tuple-element.42.cum_ref, ...), custom_call_target="tpu_custom_call" | custom-call | flops 500000000 | bytes 5000000 | tf_op jit(solution)/shard_map/pallas_call | solution.py:401
  89.9 2.3 %shard_map.139 = (bf16[256,1024]{1,0:T(8,128)(2,1)}, bf16[256,1024]{1,0:T(8,128)(2,1)}, f32[8,256]{1,0:T(8,128)}, f32[1,1024]{1,0:T(1,128)}) custom-call(bf16[256,1024]{1,0:T(8,128)(2,1)S(1)} %copy-done, bf16[256,1024]{1,0:T(8,128)(2,1)S(1)} %copy-done.1, f32[256,8]{1,0:T(8,128)S(1)} %get-tuple-element.42.cum_ref, ...), custom_call_target="tpu_custom_call" | custom-call | flops 500000000 | bytes 5000000 | tf_op jit(solution)/shard_map/pallas_call | solution.py:401
  (14 shorter events, 0.0 us)
Async XLA Ops:
  0.6 0.7 copy-start.6
  3.5 4.4 %collective-permute-start = (bf16[4,136,128]{2,1,0:T(8,128)(2,1)S(1)}, bf16[4,136,128]{2,1,0:T(8,128)(2,1)S(1)}, u32[]{:S(2)}, u32[]{:S(2)}) collective-permute-start(bf16[4,136,128]{2,1,0:T(8,128)(2,1)S(1)} %get-tuple-element.49), channel_id=1, source_target_pairs={{0,4},{4,0},{1,5},{5,1},{2,6},{6,2},{3,7},{7,3},{8,12},{12,8},{9,1... | collective-permute-start | bytes 417800 | tf_op jit(solution)/shard_map/ppermute | solution.py:417
  7.8 36.5 %copy-start.2 = (bf16[256,1024]{1,0:T(8,128)(2,1)S(1)}, bf16[256,1024]{1,0:T(8,128)(2,1)}, u32[]{:S(2)}) copy-start(bf16[256,1024]{1,0:T(8,128)(2,1)} %q_ref.3) | copy-start | bytes 1572868
  7.9 36.3 %copy-start.1 = (bf16[256,1024]{1,0:T(8,128)(2,1)S(1)}, bf16[256,1024]{1,0:T(8,128)(2,1)}, u32[]{:S(2)}) copy-start(bf16[256,1024]{1,0:T(8,128)(2,1)} %v_ref.5) | copy-start | bytes 1572868
  26.6 17.7 %copy-start = (bf16[256,1024]{1,0:T(8,128)(2,1)S(1)}, bf16[256,1024]{1,0:T(8,128)(2,1)}, u32[]{:S(2)}) copy-start(bf16[256,1024]{1,0:T(8,128)(2,1)} %k_ref.5) | copy-start | bytes 1572868
  41.3 4.4 %collective-permute-start.1 = (bf16[4,128,128]{2,1,0:T(8,128)(2,1)S(1)}, bf16[4,128,128]{2,1,0:T(8,128)(2,1)S(1)}, u32[]{:S(2)}, u32[]{:S(2)}) collective-permute-start(bf16[4,128,128]{2,1,0:T(8,128)(2,1)S(1)} %get-tuple-element.52), channel_id=1, source_target_pairs={{0,4},{4,0},{1,5},{5,1},{2,6},{6,2},{3,7},{7,3},{8,12},{12,8},{9,1... | collective-permute-start | bytes 393224 | tf_op jit(solution)/shard_map/ppermute | solution.py:417
  44.3 1.0 %copy-start.3 = (bf16[256,1024]{1,0:T(8,128)(2,1)S(1)}, bf16[256,1024]{1,0:T(8,128)(2,1)}, u32[]{:S(2)}) copy-start(bf16[256,1024]{1,0:T(8,128)(2,1)} %cot_ref.3) | copy-start | bytes 1572868
  44.3 1.0 %copy-start.4 = (f32[1024]{0:T(1024)S(1)}, f32[1024]{0:T(1024)}, u32[]{:S(2)}) copy-start(f32[1024]{0:T(1024)} %param.11) | copy-start | bytes 12292
  44.3 1.2 %copy-start.5 = (bf16[256,1024]{1,0:T(8,128)(2,1)S(1)}, bf16[256,1024]{1,0:T(8,128)(2,1)}, u32[]{:S(2)}) copy-start(bf16[256,1024]{1,0:T(8,128)(2,1)} %gate_ref.1) | copy-start | bytes 1572868
  46.3 3.9 %collective-permute-start.4 = (f32[8,256]{1,0:T(8,128)S(1)}, f32[8,256]{1,0:T(8,128)S(1)}, u32[]{:S(2)}, u32[]{:S(2)}) collective-permute-start(f32[8,256]{1,0:T(8,128)S(1)} %get-tuple-element.54.sums0_ref), channel_id=1, source_target_pairs={{0,3},{1,2},{2,1},{3,0},{4,7},{5,6},{6,5},{7,4},{8,11},{9,10},{10,... | collective-permute-start | bytes 24584 | tf_op jit(solution)/shard_map/ppermute | solution.py:479
  49.1 4.0 %collective-permute-start.3 = (f32[8,256]{1,0:T(8,128)S(1)}, f32[8,256]{1,0:T(8,128)S(1)}, u32[]{:S(2)}, u32[]{:S(2)}) collective-permute-start(f32[8,256]{1,0:T(8,128)S(1)} %get-tuple-element.54.sums0_ref), channel_id=1, source_target_pairs={{0,2},{1,3},{2,0},{3,1},{4,6},{5,7},{6,4},{7,5},{8,10},{9,11},{10,... | collective-permute-start | bytes 24584 | tf_op jit(solution)/shard_map/ppermute | solution.py:479
  49.4 3.7 %collective-permute-start.2 = (f32[8,256]{1,0:T(8,128)S(1)}, f32[8,256]{1,0:T(8,128)S(1)}, u32[]{:S(2)}, u32[]{:S(2)}) collective-permute-start(f32[8,256]{1,0:T(8,128)S(1)} %get-tuple-element.54.sums0_ref), channel_id=1, source_target_pairs={{0,1},{1,0},{2,3},{3,2},{4,5},{5,4},{6,7},{7,6},{8,9},{9,8},{10,11... | collective-permute-start | bytes 24584 | tf_op jit(solution)/shard_map/ppermute | solution.py:479
  53.9 2.8 %collective-permute-start.5 = (f32[4,136,128]{2,1,0:T(8,128)S(1)}, f32[4,136,128]{2,1,0:T(8,128)S(1)}, u32[]{:S(2)}, u32[]{:S(2)}) collective-permute-start(f32[4,136,128]{2,1,0:T(8,128)S(1)} %get-tuple-element.55), channel_id=1, source_target_pairs={{0,4},{4,0},{1,5},{5,1},{2,6},{6,2},{3,7},{7,3},{8,12},{12,8},{9,1... | collective-permute-start | bytes 835592 | tf_op jit(solution)/shard_map/ppermute | solution.py:417
  84.4 5.4 %collective-permute-start.6 = (bf16[4,136,128]{2,1,0:T(8,128)(2,1)S(1)}, bf16[4,136,128]{2,1,0:T(8,128)(2,1)S(1)}, u32[]{:S(2)}, u32[]{:S(2)}) collective-permute-start(bf16[4,136,128]{2,1,0:T(8,128)(2,1)S(1)} %get-tuple-element.71), channel_id=1, source_target_pairs={{0,4},{4,0},{1,5},{5,1},{2,6},{6,2},{3,7},{7,3},{8,12},{12,8},{9,1... | collective-permute-start | bytes 417800 | tf_op jit(solution)/shard_map/ppermute | solution.py:417

commit v5 on v4

--- a/solution.py
+++ b/solution.py
@@ -265,22 +265,34 @@
     upstream_ref[...] = cot_ref[...].astype(F32) * opened * gain_ref[...]
 
 
+def put_pairs(core, half, pairs_ref, mine_ref, got_ref):
+    pairs = half // 2
+    empty = jnp.zeros((2 * pairs, HD, HD), BF16)
+    pairs_ref[:, :HD, HD:] = empty
+    pairs_ref[:, HD:, :HD] = empty
+    for h in range(half):
+        place = slice((h % 2) * HD, (h % 2 + 1) * HD)
+        pairs_ref[core * pairs + h // 2, place, place] = mine_ref[h, :HD]
+        pairs_ref[(1 - core) * pairs + h // 2, place, place] = got_ref[h, :HD]
+
+
 def attention_kernel(
     heads, decayed_ref, intra_ref, upstream_ref, mine_ref, got_ref, attn_ref, prior_ref, sums_ref
 ):
     length = decayed_ref.shape[0]
     core = lax.axis_index("core")
     half = heads // 2
-    prior_ref[pl.ds(core * half, half)] = mine_ref[...]
-    prior_ref[pl.ds((1 - core) * half, half)] = got_ref[...]
+    put_pairs(core, half, prior_ref, mine_ref, got_ref)
     squares = jnp.zeros((length, HD), F32)
     cross = jnp.zeros((length, HD), F32)
-    for h in range(heads):
-        cols = slice(h * HD, (h + 1) * HD)
-        attn = dot(decayed_ref[:, cols], prior_ref[h]) + intra_ref[:, cols]
-        attn_ref[:, cols] = attn
-        squares = squares + attn * attn
-        cross = cross + upstream_ref[:, cols] * attn
+    for pair in range(half):
+        wide = slice(2 * pair * HD, 2 * (pair + 1) * HD)
+        attn = dot(decayed_ref[:, wide], prior_ref[pair]) + intra_ref[:, wide]
+        attn_ref[:, wide] = attn
+        square = attn * attn
+        product = upstream_ref[:, wide] * attn
+        squares = squares + square[:, :HD] + square[:, HD:]
+        cross = cross + product[:, :HD] + product[:, HD:]
     sums_ref[...] = jnp.concatenate(
         [
             jnp.sum(squares.T, axis=0, keepdims=True),
@@ -335,10 +347,13 @@
 
 def query_gradient_kernel(
     heads, q_ref, k_ref, v_ref, cum_ref, cumt_ref, grad_ref, prior_ref, weights_ref,
-    gq_hbm, gk_ref, gv_ref, gq_ref, mixed_ref, sem,
+    gq_hbm, gk_ref, gv_ref, gq_ref, mixed_ref, far_ref, sem,
 ):
     cum = cum_ref[...]
     grown = jnp.exp(cum)
+    for pair in range(heads // 2):
+        wide = slice(2 * pair * HD, 2 * (pair + 1) * HD)
+        far_ref[:, wide] = dot(grad_ref[:, wide], prior_ref[pair], (1, 1))
     for h in range(heads):
         cols = slice(h * HD, (h + 1) * HD)
         grad = grad_ref[:, cols]
@@ -346,7 +361,7 @@
         mixed = masked_bf(masks, dot(grad, v_ref[:, cols], (1, 1)))
         mixed_ref[h] = mixed
         gq = dot(mixed, k_ref[:, cols])
-        gq = gq + grown[:, h : h + 1] * dot(grad, prior_ref[h], (1, 1))
+        gq = gq + grown[:, h : h + 1] * far_ref[:, cols]
         gq_ref[:, cols] = gq.astype(BF16)
     copy = pltpu.make_async_copy(gq_ref, gq_hbm, sem)
     copy.start()
@@ -364,8 +379,7 @@
     length = k_ref.shape[0]
     half = heads // 2
     core = lax.axis_index("core")
-    later_ref[pl.ds(core * half, half)] = mine_ref[:, :HD]
-    later_ref[pl.ds((1 - core) * half, half)] = got_ref[:, :HD]
+    put_pairs(core, half, later_ref, mine_ref, got_ref)
     cum = cum_ref[...]
     last = cum[length - 1 : length]
     lane = lax.broadcasted_iota(jnp.int32, (length, HD), 1)
@@ -374,15 +388,20 @@
     changes = jnp.zeros((length, HD), F32)
     for h in range(heads):
         cols = slice(h * HD, (h + 1) * HD)
-        k, v, grad, later = k_ref[:, cols], v_ref[:, cols], grad_ref[:, cols], later_ref[h]
+        k, grad = k_ref[:, cols], grad_ref[:, cols]
+        if h % 2 == 0:
+            wide = slice(h * HD, (h + 2) * HD)
+            value_pulls = dot(v_ref[:, wide], later_ref[h // 2], (1, 1))
+            key_pulls = dot(k_ref[:, wide], later_ref[h // 2])
+        at = slice((h % 2) * HD, (h % 2 + 1) * HD)
         mine, got = mine_ref[h % half, HD:], got_ref[h % half, HD:]
         own = core == h // half
         ggain_ref[:, cols] = one_of(own, joined_rows(mine), joined_rows(got))
         fade = fades[:, h : h + 1]
-        pull = fade * dot(v, later, (1, 1))
+        pull = fade * value_pulls[:, at]
         gk_part = gk_part_ref[:, cols]
         gk_ref[:, cols] = (gk_part + pull).astype(BF16)
-        gv_ref[:, cols] = (gv_part_ref[:, cols] + fade * dot(k, later)).astype(BF16)
+        gv_ref[:, cols] = (gv_part_ref[:, cols] + fade * key_pulls[:, at]).astype(BF16)
         key = k.astype(F32)
         pulled = key * pull
         meet = one_of(own, joined_rows(mine, 1), joined_rows(got, 1))
@@ -431,6 +450,7 @@
     tokens, tokens32 = ((length, width), BF16), ((length, width), F32)
     square = ((heads, length, length), BF16)
     held = pltpu.VMEM((heads, length, HD), BF16)
+    pair_state = ((half, 2 * HD, 2 * HD), BF16)
     local, theirs, cum, cumt = local_call(
         functools.partial(local_state_kernel, heads),
         [(state, BF16), (carried, BF16), ((length, heads), F32), ((heads, length), F32)],
@@ -471,7 +491,7 @@
     )
     attn, prior, sums = local_call(
         functools.partial(attention_kernel, heads),
-        [tokens32, (state, BF16), ((8, length), F32)],
+        [tokens32, pair_state, ((8, length), F32)],
         (decayed, intra, upstream, mine, swap(theirs)),
         WORK, WORK // 100,
     )
@@ -515,7 +535,7 @@
         [tokens, tokens32, tokens32],
         (queries, key_rows, value_rows, cum, cumt, grad, prior, weights),
         WORK, WORK // 100,
-        [pltpu.VMEM(*tokens), pltpu.VMEM(*square), pltpu.SemaphoreType.DMA],
+        [pltpu.VMEM(*tokens), pltpu.VMEM(*square), pltpu.VMEM(*tokens32), pltpu.SemaphoreType.DMA],
         far_out=(0,),
     )
     grad_k, grad_v, grad_decay, grad_gain = local_call(
@@ -523,7 +543,7 @@
         [tokens, tokens, ((heads, length), F32), ((1, width), F32)],
         (key_rows, value_rows, cum, attn, grad, gk_part, gv_part, mine, swap(theirs)),
         WORK, WORK // 100,
-        [pltpu.VMEM(state, BF16)],
+        [pltpu.VMEM(*pair_state)],
     )
     return attended, grad_q, grad_k, grad_v, grad_gate, grad_decay.T, grad_gain.reshape(width)
 

time: 92.5 us -> 92.4 us (level)
  no operation moved by 1% of the time
where the time goes in v5:
time: 92.4 us; the launch traced here: 92.1 us
  blocking collectives  60.3 us (65%)
  starting transfers between devices  14.6 us (16%)
  Pallas kernels  11.2 us (12%)
  waiting for transfers between devices  4.33 us (5%)
  local copies, waits for them, and re-layouts  0.93 us (1%)
    all_to_all x4, blocking collectives, exchange(): return lax.all_to_all(payload, ('x', 'z'), 0, 0, tiled=True)  60.3 us
    pallas_call x14, Pallas kernels, local_call(): pl.pallas_call(kernel, out_shape=[jax.ShapeDtypeStruct(shape, kind) for s...  11.2 us
    ppermute x4, starting transfers between devices, swap(): return lax.ppermute(value, 'core', [(0, 1), (1, 0)])  11.1 us
    ppermute x3, starting transfers between devices, per_device(): lax.ppermute(sums, 'head', [(i, i ^ step) for i in range(size)])  3.49 us
    ppermute x3, waiting for transfers between devices, per_device(): lax.ppermute(sums, 'head', [(i, i ^ step) for i in range(size)])  3.33 us
  transfers between devices with their start and end apart: 7, of which 3 were waited for; matrix products, arithmetic and copies ran while one was open for 0% of the time, Pallas kernels for 5%

profile of v5, /device:TPU:1, one launch (start us, length us, event | category | flops | bytes accessed | tf_op | source)
XLA Modules:
  0.0 92.1 jit_solution(8349774673711514226)
XLA Ops:
  0.6 0.7 copy-done.6
  1.3 2.1 %shard_map.126 = (bf16[8,128,128]{2,1,0:T(8,128)(2,1)S(1)}, bf16[4,136,128]{2,1,0:T(8,128)(2,1)S(1)}, f32[256,8]{1,0:T(8,128)S(1)}, f32[8,256]{1,0:T(8,128)S(1)}) custom-call(bf16[256,1024]{1,0:T(8,128)(2,1)} %k_ref.5, bf16[256,1024]{1,0:T(8,128)(2,1)} %v_ref.5, f32[8,256]{1,0:T(8,128)S(1)} %bitcast.9), custom_call_target="tpu_custom_call" | custom-call | flops 500000000 | bytes 5000000 | tf_op jit(solution)/shard_map/pallas_call | solution.py:420
  3.5 3.4 %collective-permute-start = (bf16[4,136,128]{2,1,0:T(8,128)(2,1)S(1)}, bf16[4,136,128]{2,1,0:T(8,128)(2,1)S(1)}, u32[]{:S(2)}, u32[]{:S(2)}) collective-permute-start(bf16[4,136,128]{2,1,0:T(8,128)(2,1)S(1)} %get-tuple-element.49), channel_id=1, source_target_pairs={{0,4},{4,0},{1,5},{5,1},{2,6},{6,2},{3,7},{7,3},{8,12},{12,8},{9,1... | collective-permute-start | bytes 417800 | tf_op jit(solution)/shard_map/ppermute | solution.py:436
  6.8 1.0 %collective-permute-done.got_ref.got_state_ref = bf16[4,136,128]{2,1,0:T(8,128)(2,1)S(1)} collective-permute-done((bf16[4,136,128]{2,1,0:T(8,128)(2,1)S(1)}, bf16[4,136,128]{2,1,0:T(8,128)(2,1)S(1)}, u32[]{:S(2)}, u32[]{:S(2)}) %collective-permute-start) | collective-permute-done | bytes 139296 | tf_op jit(solution)/shard_map/ppermute | solution.py:436
  7.8 0.1 shard_map.129
  7.9 0.0 copy-start.1
  8.0 18.6 %all_to_all.20.pay_ref = bf16[32,24,128]{2,1,0:T(8,128)(2,1)S(1)} all-to-all(bf16[32,24,128]{2,1,0:T(8,128)(2,1)S(1)} %shard_map.129), channel_id=1, replica_groups=mesh['x'=4,'z'=8,'core'=2,'head'=4] {'x','z'}, dimensions={0} | all-to-all | bytes 393216 | tf_op jit(solution)/shard_map/all_to_all | solution.py:432
  26.6 0.1 shard_map.130
  26.7 14.5 %all_to_all.21 = bf16[32,16,128]{2,1,0:T(8,128)(2,1)S(1)} all-to-all(bf16[32,16,128]{2,1,0:T(8,128)(2,1)S(1)} %get-tuple-element.50), channel_id=1, replica_groups=mesh['x'=4,'z'=8,'core'=2,'head'=4] {'x','z'}, dimensions={0} | all-to-all | bytes 262144 | tf_op jit(solution)/shard_map/all_to_all | solution.py:432
  41.2 0.1 shard_map.131
  41.3 2.9 %collective-permute-start.1 = (bf16[4,128,128]{2,1,0:T(8,128)(2,1)S(1)}, bf16[4,128,128]{2,1,0:T(8,128)(2,1)S(1)}, u32[]{:S(2)}, u32[]{:S(2)}) collective-permute-start(bf16[4,128,128]{2,1,0:T(8,128)(2,1)S(1)} %get-tuple-element.52), channel_id=1, source_target_pairs={{0,4},{4,0},{1,5},{5,1},{2,6},{6,2},{3,7},{7,3},{8,12},{12,8},{9,1... | collective-permute-start | bytes 393224 | tf_op jit(solution)/shard_map/ppermute | solution.py:436
  44.3 1.0 %shard_map.127 = (f32[256,1024]{1,0:T(8,128)S(1)}, bf16[8,256,256]{2,1,0:T(8,128)(2,1)S(1)}, bf16[256,1024]{1,0:T(8,128)(2,1)S(1)}) custom-call(bf16[256,1024]{1,0:T(8,128)(2,1)S(1)} %copy-done.3, bf16[256,1024]{1,0:T(8,128)(2,1)S(1)} %copy-done, bf16[256,1024]{1,0:T(8,128)(2,1)S(1)} %copy-done.1, f32[256,8]{1,0:T(8,128)S(1)} %get-tuple-element.42.cum_ref, ...), custom_call_target="tpu_custom_call" | custom-call | flops 500000000 | bytes 5000000 | tf_op jit(solution)/shard_map/pallas_call | solution.py:420
  45.3 0.0 copy-done.2
  45.3 0.2 copy-done.5
  45.5 0.2 shard_map.128
  45.8 0.6 shard_map.132
  46.3 2.8 %collective-permute-start.4 = (f32[8,256]{1,0:T(8,128)S(1)}, f32[8,256]{1,0:T(8,128)S(1)}, u32[]{:S(2)}, u32[]{:S(2)}) collective-permute-start(f32[8,256]{1,0:T(8,128)S(1)} %get-tuple-element.54.sums0_ref), channel_id=1, source_target_pairs={{0,3},{1,2},{2,1},{3,0},{4,7},{5,6},{6,5},{7,4},{8,11},{9,10},{10,... | collective-permute-start | bytes 24584 | tf_op jit(solution)/shard_map/ppermute | solution.py:499
  49.1 0.4 collective-permute-start.3
  49.5 0.3 collective-permute-start.2
  49.8 0.4 collective-permute-done.4.sums3_ref
  50.2 3.0 %collective-permute-done.3.sums2_ref = f32[8,256]{1,0:T(8,128)S(1)} collective-permute-done((f32[8,256]{1,0:T(8,128)S(1)}, f32[8,256]{1,0:T(8,128)S(1)}, u32[]{:S(2)}, u32[]{:S(2)}) %collective-permute-start.3) | collective-permute-done | bytes 8224 | tf_op jit(solution)/shard_map/ppermute | solution.py:499
  53.1 0.8 shard_map.133
  53.9 1.6 %collective-permute-start.5 = (f32[4,136,128]{2,1,0:T(8,128)S(1)}, f32[4,136,128]{2,1,0:T(8,128)S(1)}, u32[]{:S(2)}, u32[]{:S(2)}) collective-permute-start(f32[4,136,128]{2,1,0:T(8,128)S(1)} %get-tuple-element.55), channel_id=1, source_target_pairs={{0,4},{4,0},{1,5},{5,1},{2,6},{6,2},{3,7},{7,3},{8,12},{12,8},{9,1... | collective-permute-start | bytes 835592 | tf_op jit(solution)/shard_map/ppermute | solution.py:436
  55.5 1.2 %shard_map.134 = (bf16[256,1024]{1,0:T(8,128)(2,1)}, bf16[256,1024]{1,0:T(8,128)(2,1)}) custom-call(f32[256,1024]{1,0:T(8,128)S(1)} %get-tuple-element.45.opened_ref, f32[256,1024]{1,0:T(8,128)S(1)} %get-tuple-element.46.upstream_ref, f32[1,1024]{1,0:T(1,128)S(1)} %bitcast.8, f32[256,1024]{1,0:T(8,128)S(1)} %get-tuple-element.53.attn_ref, ...), custom_call_target="tpu_custom_call" | custom-call | flops 500000000 | bytes 5000000 | tf_op jit(solution)/shard_map/pallas_call | solution.py:420
  56.8 0.1 shard_map.136
  56.9 12.5 %all_to_all.22.pay_ref = bf16[32,24,128]{2,1,0:T(8,128)(2,1)S(1)} all-to-all(bf16[32,24,128]{2,1,0:T(8,128)(2,1)S(1)} %shard_map.136), channel_id=1, replica_groups=mesh['x'=4,'z'=8,'core'=2,'head'=4] {'x','z'}, dimensions={0} | all-to-all | bytes 393216 | tf_op jit(solution)/shard_map/all_to_all | solution.py:432
  69.4 0.2 shard_map.137
  69.6 14.6 %all_to_all.23.back_ref = bf16[32,24,128]{2,1,0:T(8,128)(2,1)S(1)} all-to-all(bf16[32,24,128]{2,1,0:T(8,128)(2,1)S(1)} %shard_map.137), channel_id=1, replica_groups=mesh['x'=4,'z'=8,'core'=2,'head'=4] {'x','z'}, dimensions={0} | all-to-all | bytes 393216 | tf_op jit(solution)/shard_map/all_to_all | solution.py:432
  84.2 0.2 shard_map.138
  84.5 3.3 %collective-permute-start.6 = (bf16[4,136,128]{2,1,0:T(8,128)(2,1)S(1)}, bf16[4,136,128]{2,1,0:T(8,128)(2,1)S(1)}, u32[]{:S(2)}, u32[]{:S(2)}) collective-permute-start(bf16[4,136,128]{2,1,0:T(8,128)(2,1)S(1)} %get-tuple-element.71), channel_id=1, source_target_pairs={{0,4},{4,0},{1,5},{5,1},{2,6},{6,2},{3,7},{7,3},{8,12},{12,8},{9,1... | collective-permute-start | bytes 417800 | tf_op jit(solution)/shard_map/ppermute | solution.py:436
  87.7 2.1 %shard_map.135 = (bf16[256,1024]{1,0:T(8,128)(2,1)}, f32[256,1024]{1,0:T(8,128)S(1)}, f32[256,1024]{1,0:T(8,128)S(1)}) custom-call(bf16[256,1024]{1,0:T(8,128)(2,1)S(1)} %copy-done.3, bf16[256,1024]{1,0:T(8,128)(2,1)S(1)} %copy-done, bf16[256,1024]{1,0:T(8,128)(2,1)S(1)} %copy-done.1, f32[256,8]{1,0:T(8,128)S(1)} %get-tuple-element.42.cum_ref, ...), custom_call_target="tpu_custom_call" | custom-call | flops 500000000 | bytes 5000000 | tf_op jit(solution)/shard_map/pallas_call | solution.py:420
  89.8 2.3 %shard_map.139 = (bf16[256,1024]{1,0:T(8,128)(2,1)}, bf16[256,1024]{1,0:T(8,128)(2,1)}, f32[8,256]{1,0:T(8,128)}, f32[1,1024]{1,0:T(1,128)}) custom-call(bf16[256,1024]{1,0:T(8,128)(2,1)S(1)} %copy-done, bf16[256,1024]{1,0:T(8,128)(2,1)S(1)} %copy-done.1, f32[256,8]{1,0:T(8,128)S(1)} %get-tuple-element.42.cum_ref, ...), custom_call_target="tpu_custom_call" | custom-call | flops 500000000 | bytes 5000000 | tf_op jit(solution)/shard_map/pallas_call | solution.py:420
  (14 shorter events, 0.0 us)
Async XLA Ops:
  0.6 0.7 copy-start.6
  3.5 4.4 %collective-permute-start = (bf16[4,136,128]{2,1,0:T(8,128)(2,1)S(1)}, bf16[4,136,128]{2,1,0:T(8,128)(2,1)S(1)}, u32[]{:S(2)}, u32[]{:S(2)}) collective-permute-start(bf16[4,136,128]{2,1,0:T(8,128)(2,1)S(1)} %get-tuple-element.49), channel_id=1, source_target_pairs={{0,4},{4,0},{1,5},{5,1},{2,6},{6,2},{3,7},{7,3},{8,12},{12,8},{9,1... | collective-permute-start | bytes 417800 | tf_op jit(solution)/shard_map/ppermute | solution.py:436
  7.8 36.5 %copy-start.3 = (bf16[256,1024]{1,0:T(8,128)(2,1)S(1)}, bf16[256,1024]{1,0:T(8,128)(2,1)}, u32[]{:S(2)}) copy-start(bf16[256,1024]{1,0:T(8,128)(2,1)} %q_ref.3) | copy-start | bytes 1572868
  7.9 36.3 %copy-start.1 = (bf16[256,1024]{1,0:T(8,128)(2,1)S(1)}, bf16[256,1024]{1,0:T(8,128)(2,1)}, u32[]{:S(2)}) copy-start(bf16[256,1024]{1,0:T(8,128)(2,1)} %v_ref.5) | copy-start | bytes 1572868
  26.6 17.7 %copy-start = (bf16[256,1024]{1,0:T(8,128)(2,1)S(1)}, bf16[256,1024]{1,0:T(8,128)(2,1)}, u32[]{:S(2)}) copy-start(bf16[256,1024]{1,0:T(8,128)(2,1)} %k_ref.5) | copy-start | bytes 1572868
  41.3 4.4 %collective-permute-start.1 = (bf16[4,128,128]{2,1,0:T(8,128)(2,1)S(1)}, bf16[4,128,128]{2,1,0:T(8,128)(2,1)S(1)}, u32[]{:S(2)}, u32[]{:S(2)}) collective-permute-start(bf16[4,128,128]{2,1,0:T(8,128)(2,1)S(1)} %get-tuple-element.52), channel_id=1, source_target_pairs={{0,4},{4,0},{1,5},{5,1},{2,6},{6,2},{3,7},{7,3},{8,12},{12,8},{9,1... | collective-permute-start | bytes 393224 | tf_op jit(solution)/shard_map/ppermute | solution.py:436
  44.3 1.0 %copy-start.2 = (bf16[256,1024]{1,0:T(8,128)(2,1)S(1)}, bf16[256,1024]{1,0:T(8,128)(2,1)}, u32[]{:S(2)}) copy-start(bf16[256,1024]{1,0:T(8,128)(2,1)} %cot_ref.3) | copy-start | bytes 1572868
  44.3 1.0 %copy-start.4 = (f32[1024]{0:T(1024)S(1)}, f32[1024]{0:T(1024)}, u32[]{:S(2)}) copy-start(f32[1024]{0:T(1024)} %param.11) | copy-start | bytes 12292
  44.3 1.2 %copy-start.5 = (bf16[256,1024]{1,0:T(8,128)(2,1)S(1)}, bf16[256,1024]{1,0:T(8,128)(2,1)}, u32[]{:S(2)}) copy-start(bf16[256,1024]{1,0:T(8,128)(2,1)} %gate_ref.1) | copy-start | bytes 1572868
  46.3 3.9 %collective-permute-start.4 = (f32[8,256]{1,0:T(8,128)S(1)}, f32[8,256]{1,0:T(8,128)S(1)}, u32[]{:S(2)}, u32[]{:S(2)}) collective-permute-start(f32[8,256]{1,0:T(8,128)S(1)} %get-tuple-element.54.sums0_ref), channel_id=1, source_target_pairs={{0,3},{1,2},{2,1},{3,0},{4,7},{5,6},{6,5},{7,4},{8,11},{9,10},{10,... | collective-permute-start | bytes 24584 | tf_op jit(solution)/shard_map/ppermute | solution.py:499
  49.1 4.0 %collective-permute-start.3 = (f32[8,256]{1,0:T(8,128)S(1)}, f32[8,256]{1,0:T(8,128)S(1)}, u32[]{:S(2)}, u32[]{:S(2)}) collective-permute-start(f32[8,256]{1,0:T(8,128)S(1)} %get-tuple-element.54.sums0_ref), channel_id=1, source_target_pairs={{0,2},{1,3},{2,0},{3,1},{4,6},{5,7},{6,4},{7,5},{8,10},{9,11},{10,... | collective-permute-start | bytes 24584 | tf_op jit(solution)/shard_map/ppermute | solution.py:499
  49.5 3.7 %collective-permute-start.2 = (f32[8,256]{1,0:T(8,128)S(1)}, f32[8,256]{1,0:T(8,128)S(1)}, u32[]{:S(2)}, u32[]{:S(2)}) collective-permute-start(f32[8,256]{1,0:T(8,128)S(1)} %get-tuple-element.54.sums0_ref), channel_id=1, source_target_pairs={{0,1},{1,0},{2,3},{3,2},{4,5},{5,4},{6,7},{7,6},{8,9},{9,8},{10,11... | collective-permute-start | bytes 24584 | tf_op jit(solution)/shard_map/ppermute | solution.py:499
  53.9 2.8 %collective-permute-start.5 = (f32[4,136,128]{2,1,0:T(8,128)S(1)}, f32[4,136,128]{2,1,0:T(8,128)S(1)}, u32[]{:S(2)}, u32[]{:S(2)}) collective-permute-start(f32[4,136,128]{2,1,0:T(8,128)S(1)} %get-tuple-element.55), channel_id=1, source_target_pairs={{0,4},{4,0},{1,5},{5,1},{2,6},{6,2},{3,7},{7,3},{8,12},{12,8},{9,1... | collective-permute-start | bytes 835592 | tf_op jit(solution)/shard_map/ppermute | solution.py:436
  84.5 5.4 %collective-permute-start.6 = (bf16[4,136,128]{2,1,0:T(8,128)(2,1)S(1)}, bf16[4,136,128]{2,1,0:T(8,128)(2,1)S(1)}, u32[]{:S(2)}, u32[]{:S(2)}) collective-permute-start(bf16[4,136,128]{2,1,0:T(8,128)(2,1)S(1)} %get-tuple-element.71), channel_id=1, source_target_pairs={{0,4},{4,0},{1,5},{5,1},{2,6},{6,2},{3,7},{7,3},{8,12},{12,8},{9,1... | collective-permute-start | bytes 417800 | tf_op jit(solution)/shard_map/ppermute | solution.py:436
